TPU v7x, 32 devices: a whole 2x2x4 slice. The times are simulated.
32 devices in a mesh: groups: 2 (over x), blk: 16 (over z, y, core).
Axes of the slice: x: 2, y: 2, z: 4, core: 2. Of those that a mesh axis runs over, the one named last changes fastest.
Arguments:
- pop_cells: bfloat16 [2048, 1024], P('blk', 'groups'), parts along dimension 1, may hold values from 0.0009994507 to 1
- cell_map: int32 [512], replicated, may hold values from 0 to 255, never falling along the last dimension, each value on 1 to 4 neighbouring positions
- line_level: int32 [524288], P('blk'), may hold values from 0 to 2047
- line_strength: float32 [524288], P('blk'), may hold values from 0.001 to 1
- inst_wave: float32 [129], replicated, may hold values from 0.002 to 0.02
- inst_slit: float32 [9], replicated, may hold values from 0.05 to 0.25
Outputs:
- image: float32 [512, 2048], P(('groups', 'blk')), parts along dimension 0
There are 2 independent parts, one for each index of `groups`. A program takes and returns all parts, laid end to end along the dimension named above; an argument that names none is the same for every part. Nothing has to cross between parts.
All inputs are finite; a program needn't handle non-finite values.
Results may differ from a plain program's by a relative error of at most 0.0003.
Values may be sent and summed in bfloat16 or wider, within the bound.
No kernel may reach another device: no remote copies, remote signals or barrier semaphores. Data moves between devices by JAX's collectives and lax.ppermute only.
A program may use at most 128 MiB of HBM per device.

v0:
```python
import jax
import jax.numpy as jnp
from jax import lax
from jax.sharding import PartitionSpec as P

L = 2048
CELL_DEV = 16
W_DEV = 1024
LINES_BIN = 32


def padded_2(cells, sides, width):
    for axis, dim in sides:
        count = lax.axis_size(axis)
        ends = count - 1
        head = lax.slice_in_dim(cells, 0, width, axis=dim)
        tail = lax.slice_in_dim(cells, cells.shape[dim] - width, cells.shape[dim], axis=dim)
        cells = jnp.concatenate(
            [
                lax.ppermute(tail, axis, [(i, (i + 1) % count) for i in range(ends)]),
                cells,
                lax.ppermute(head, axis, [((i + 1) % count, i) for i in range(ends)]),
            ],
            axis=dim,
        )
    return cells


def smear(padded, inst_wave):
    cells = padded.shape[0]
    width = padded.shape[1]
    outputs = (width - 128) // 8
    blocks = jnp.concatenate([inst_wave, jnp.zeros((7,), inst_wave.dtype)]).reshape(17, 8)
    parts = jnp.transpose(padded.reshape(cells, width // 8, 8), (2, 0, 1))
    total = jnp.zeros((cells, outputs), padded.dtype)
    for block_index in range(17):
        window = parts[:, :, block_index : block_index + outputs]
        total = total + jnp.einsum(
            "i,icb->cb", blocks[block_index], window, precision=lax.Precision.HIGHEST
        )
    return total


def slit_blur(smeared, inst_slit):
    cells = smeared.shape[0]
    padded = jnp.pad(smeared, ((4, 4), (0, 0)))
    total = inst_slit[0] * padded[0:cells]
    for tap_index in range(1, 9):
        total = total + inst_slit[tap_index] * padded[tap_index : tap_index + cells]
    return total


def body(pop_cells, cell_map, line_level, line_strength, inst_wave, inst_slit):
    cells = lax.axis_size("blk") * CELL_DEV
    line_count = line_level.shape[0]
    line_bins = jnp.arange(line_count, dtype=jnp.int32) // LINES_BIN
    emission_t = (
        jnp.zeros((W_DEV, L), jnp.float32)
        .at[line_bins, line_level]
        .add(line_strength)
        .astype(jnp.bfloat16)
    )
    onehot = (cell_map[:, None] == jnp.arange(cells, dtype=jnp.int32)[None, :]).astype(jnp.bfloat16)
    slit_pop = jnp.dot(pop_cells, onehot, preferred_element_type=jnp.float32).astype(jnp.bfloat16)
    contract_levels = (((0,), (1,)), ((), ()))
    spectrum = lax.dot_general(
        lax.all_gather(slit_pop, "blk", axis=0, tiled=True),
        emission_t,
        contract_levels,
        preferred_element_type=jnp.float32,
    )
    padded = padded_2(spectrum.astype(jnp.bfloat16), (("blk", 1),), 64).astype(spectrum.dtype)
    smeared = smear(padded, inst_wave)
    blurred = slit_blur(smeared, inst_slit)
    return lax.all_to_all(blurred, "blk", split_axis=0, concat_axis=1, tiled=True)


def solution(mesh):
    placed = (P("blk", "groups"), P(), P("blk"), P("blk"), P(), P())
    return jax.shard_map(
        body, mesh=mesh, in_specs=placed, out_specs=P(("groups", "blk"), None), check_vma=False
    )
```

profile of v0, /device:TPU:0, one launch (start us, length us, event | category | flops | bytes accessed | tf_op | source)
XLA Modules:
  0.0 255.4 jit_solution(5825756687933603950)
XLA Ops:
  6.5 0.9 copy-done
  7.4 1.7 fusion.2
  9.3 0.9 compare_select_fusion.1
  10.2 1.2 multiply_reduce_fusion
  11.4 1.3 and_reduce_fusion
  12.7 176.2 %scatter_custom_fusion = f32[2097152]{0:T(1024)} fusion(s32[32768]{0:T(1024)S(1)} %broadcast_select_fusion, f32[32768]{0:T(1024)} %param.9, f32[]{:T(128)} %constant.20.clone.1), kind=kCustom, calls=%fused_computation.1 | custom fusion | flops 32768 | bytes 8389120
  188.8 5.1 %convert_element_type.20 = bf16[2097152]{0:T(1024)(128)(2,1)} convert(f32[2097152]{0:T(1024)} %scatter_custom_fusion) | non-fusion elementwise | flops 2097152 | bytes 12582912 | tf_op jit(solution)/shard_map/convert_element_type | solution.py:61
  193.9 7.3 %reshape.90 = bf16[1024,2048]{1,0:T(8,128)(2,1)} reshape(bf16[2097152]{0:T(1024)(128)(2,1)} %convert_element_type.20) | data formatting | bytes 8388608 | tf_op jit(solution)/shard_map/convert_element_type | solution.py:61
  201.2 3.8 %convolution_convert_fusion = bf16[256,1024]{1,0:T(8,128)(2,1)S(1)} fusion(bf16[2048,256]{0,1:T(8,128)(2,1)} %all-gather.2.cloned.1.call-done, bf16[1024,2048]{1,0:T(8,128)(2,1)} %reshape.90), kind=kOutput, calls=%fused_computation.3 | convolution fusion | flops 1074003968 | bytes 5767168 | tf_op jit(solution)/shard_map/dot_general | solution.py:66
  205.1 2.3 collective-permute-start
  207.4 1.5 collective-permute-start.1
  208.9 0.7 fusion.81
  209.6 3.2 %collective-permute-done.1 = bf16[256,64]{1,0:T(8,128)(2,1)S(1)} collective-permute-done((bf16[256,64]{1,0:T(8,128)(2,1)S(1)}, bf16[256,64]{1,0:T(8,128)(2,1)S(1)}, u32[]{:S(2)}, u32[]{:S(2)}) %collective-permute-start.1) | collective-permute-done | bytes 32800 | tf_op jit(solution)/shard_map/ppermute | solution.py:22
  214.2 0.6 fusion.43
  215.5 0.6 fusion.39
  216.1 0.6 fusion.37
  217.4 0.6 fusion.33
  219.3 0.6 fusion.27
  220.6 0.6 fusion.23
  221.2 0.6 fusion.21
  222.5 0.6 fusion.17
  226.3 5.8 %multiply_add_fusion = f32[256,128]{1,0:T(8,128)S(1)} fusion(f32[256,128]{1,0:T(8,128)S(1)} %bitcast_add_fusion, f32[]{:T(128)} %bitcast.47, f32[]{:T(128)} %bitcast.46, f32[]{:T(128)} %bitcast.45, f32[]{:T(128)} %bitcast.44, f32[]{:T(128)} %bitcast.43, f32[]{:T(128)} %bitcast.42, f32[]{:T(128)} %bitcast.41, f32[]{:T(128)} %bitcast.40, f32[]{:T(128)} %bitcast), kind=kLoop, calls=%fused_computation.37 | loop fusion | flops 557056 | bytes 262180 | tf_op jit(solution)/shard_map/add | solution.py:49
  232.1 15.9 %all_to_all.19 = f32[16,16,128]{2,1,0:T(8,128)S(1)} all-to-all(f32[16,16,128]{2,1,0:T(8,128)S(1)} %bitcast.175), channel_id=1, replica_groups=mesh['groups'=2,'blk'=16] {'blk'}, dimensions={0} | all-to-all | bytes 262144 | tf_op jit(solution)/shard_map/all_to_all | solution.py:75
  247.9 0.7 copy_bitcast_fusion
  (41 shorter events, 8.4 us)
Async XLA Ops:
  6.5 0.9 copy-start
  6.5 194.7 %all-gather.2.cloned.1.call-start = ((), (), s32[]{:S(2)}) async-start(), calls=%async_computation.1 | async-start | bytes 1114112 | tf_op jit(solution)/shard_map/all_gather | solution.py:67
  193.9 15.0 %copy-start.2 = (f32[9]{0:T(128)S(1)}, f32[9]{0:T(128)}, u32[]{:S(2)}) copy-start(f32[9]{0:T(128)} %param.11) | copy-start | bytes 112
  193.9 19.7 %copy-start.1 = (f32[129]{0:T(256)S(1)}, f32[129]{0:T(256)}, u32[]{:S(2)}) copy-start(f32[129]{0:T(256)} %param.10) | copy-start | bytes 1552
  205.1 4.5 %collective-permute-start = (bf16[256,64]{1,0:T(8,128)(2,1)S(1)}, bf16[256,64]{1,0:T(8,128)(2,1)S(1)}, u32[]{:S(2)}, u32[]{:S(2)}) collective-permute-start(bf16[256,64]{1,0:T(8,128)(2,1)S(1)} %get-tuple-element.6), channel_id=1, source_target_pairs={{0,1},{1,2},{2,3},{3,4},{4,5},{5,6},{6,7},{7,8},{8,9},{9,10},{10,1... | collective-permute-start | bytes 98312 | tf_op jit(solution)/shard_map/ppermute | solution.py:20
  207.4 5.4 %collective-permute-start.1 = (bf16[256,64]{1,0:T(8,128)(2,1)S(1)}, bf16[256,64]{1,0:T(8,128)(2,1)S(1)}, u32[]{:S(2)}, u32[]{:S(2)}) collective-permute-start(bf16[256,64]{1,0:T(8,128)(2,1)S(1)} %get-tuple-element.5), channel_id=1, source_target_pairs={{1,0},{2,1},{3,2},{4,3},{5,4},{6,5},{7,6},{8,7},{9,8},{10,9},{11,1... | collective-permute-start | bytes 98312 | tf_op jit(solution)/shard_map/ppermute | solution.py:22
Sparse Core Ops, SparseCore 0:
  9.5 39.5 all-gather.1
where the time goes:
time: 256 us; the launch traced here: 255 us
  other arithmetic  191 us (75%)
  matrix products  16 us (6%)
  blocking collectives  15.9 us (6%)
  between operations  13.8 us (5%)
  local copies, waits for them, and re-layouts  12.2 us (5%)
  starting transfers between devices  3.73 us (1%)
  waiting for transfers between devices  3.21 us (1%)
    unnamed x4, other arithmetic  179 us
    all_to_all x1, blocking collectives, body(): lax.all_to_all(blurred, 'blk', split_axis=0, concat_axis=1, tiled=True)  15.9 us
    dot_general x17, matrix products, smear(): jnp.einsum('i,icb->cb', blocks[block_index], window, precision=lax.Precis...  10.5 us
    convert_element_type x1, local copies, waits for them, and re-layouts, body(): emission_t = jnp.zeros((W_DEV, L), jnp.float32).at[line_bins, line_level]...  7.32 us
    add x1, other arithmetic, slit_blur(): total = total + inst_slit[tap_index] * padded[tap_index:tap_index + cells]  5.76 us
  transfers between devices with their start and end apart: 3, of which 1 were waited for; matrix products, arithmetic and copies ran while one was open for 75% of the time, Pallas kernels for 0%

commit v1 on v0

v1 whole, which is shorter than its diff:
```python
import functools

import jax
import jax.numpy as jnp
from jax import lax
from jax.experimental import pallas as pl
from jax.experimental.pallas import tpu as pltpu
from jax.sharding import PartitionSpec as P

L = 2048
LINES_BIN = 32
CELL_DEV = 16
SPLIT = (2, 2, 0)
LOW = 128
HIGH = L // LOW
BINS = 8
CHUNK = 256
REACH = 8
BF16 = jnp.bfloat16
F32 = jnp.float32
VMEM_LIMIT = 48 * 1024 * 1024
CONTRACT_LAST = (((1,), (1,)), ((), ()))


def two_terms(values):
    first = values.astype(BF16)
    return first, (values - first.astype(F32)).astype(BF16)


def emission_kernel(level_ref, strength_ref, wave_ref, out_ref, em_ref, *, first_chunk, chunks, unroll):
    outputs = CHUNK // BINS
    base = jnp.broadcast_to(wave_ref[...], (outputs + 2 * REACH, wave_ref.shape[1]))
    taps = pltpu.roll(base, wave_ref.shape[1] - 128, 1, stride=BINS, stride_axis=0)[:, :CHUNK]
    taps = jnp.concatenate(two_terms(taps), axis=0)
    rows = [
        (lax.broadcasted_iota(jnp.int32, (16, 128), 0) + 16 * block).astype(F32).astype(BF16)
        for block in range(LOW // 16)
    ]
    lane_bin = lax.broadcasted_iota(jnp.int32, (1, 128), 1) // LINES_BIN
    zero = jnp.zeros((16, 128), BF16)
    one = jnp.ones((16, 128), BF16)

    def spread(row):
        return jnp.broadcast_to(row.astype(F32), (16, 128)).astype(BF16)

    def half(index, part):
        level = level_ref[pl.ds(index, 1), :]
        high = spread((level // LOW) * BINS + (lane_bin + part * (128 // LINES_BIN)))
        low = spread(level % LOW)
        strength = spread(strength_ref[pl.ds(index, 1), :])
        a = jnp.concatenate([jnp.where(high == row, strength, zero) for row in rows], axis=0)
        b = jnp.concatenate([jnp.where(low == row, one, zero) for row in rows], axis=0)
        return a, b

    def group(index):
        a0, b0 = half(2 * index, 0)
        a1, b1 = half(2 * index + 1, 1)
        return lax.dot_general(
            jnp.concatenate([a0, a1], axis=1),
            jnp.concatenate([b0, b1], axis=1),
            CONTRACT_LAST,
            preferred_element_type=F32,
        )

    out_ref[...] = jnp.zeros_like(out_ref)
    groups = CHUNK // BINS
    for chunk in range(chunks):

        @pl.loop(0, groups // 2, unroll=unroll)
        def _(pair):
            index = (first_chunk + chunk) * groups + 2 * pair
            x = group(index)
            y = group(index + 1)
            place = pl.ds(pl.multiple_of(16 * pair, 16), 16)
            for h in range(HIGH):
                rows_h = slice(BINS * h, BINS * h + BINS)
                em_ref[place, h * LOW : (h + 1) * LOW] = jnp.concatenate(
                    [x[rows_h], y[rows_h]], axis=0
                ).astype(BF16)

        blurred = jnp.dot(taps, em_ref[...], preferred_element_type=F32)
        span = outputs + 2 * REACH
        out_ref[outputs * chunk : outputs * chunk + span, :] += blurred[:span] + blurred[span:]


def blurred_emission(level, strength, wave, first_chunk, chunks, unroll=4):
    outputs = CHUNK // BINS
    bins = level.size // LINES_BIN
    cost = pl.CostEstimate(
        flops=2 * chunks * CHUNK * L * (HIGH * BINS + 96), bytes_accessed=chunks * CHUNK * 256, transcendentals=0
    )
    return pl.pallas_call(
        functools.partial(emission_kernel, first_chunk=first_chunk, chunks=chunks, unroll=unroll),
        out_shape=jax.ShapeDtypeStruct((outputs * chunks + 2 * REACH, L), F32),
        scratch_shapes=[pltpu.VMEM((CHUNK, L), BF16)],
        compiler_params=pltpu.CompilerParams(vmem_limit_bytes=VMEM_LIMIT),
        cost_estimate=cost,
        name="emission",
    )(level, strength, wave)


def image_kernel(slit_ref, pop_ref, *refs, starts):
    part_refs = refs[: len(starts)]
    out_ref, e_ref, pad_ref = refs[len(starts) :]
    cells = pop_ref.shape[0]
    outputs = out_ref.shape[1] - 128
    e_ref[...] = jnp.zeros_like(e_ref)
    for start, part_ref in zip(starts, part_refs):
        e_ref[start : start + part_ref.shape[0], :] += part_ref[...]
    rows = jnp.concatenate(
        [
            e_ref[REACH : REACH + outputs, :],
            e_ref[REACH + outputs :, :],
            jnp.zeros((128 - 2 * REACH, e_ref.shape[1]), F32),
            e_ref[:REACH, :],
        ],
        axis=0,
    )
    first, second = two_terms(rows)
    smeared = lax.dot_general(pop_ref[...], first, CONTRACT_LAST, preferred_element_type=F32)
    smeared += lax.dot_general(pop_ref[...], second, CONTRACT_LAST, preferred_element_type=F32)
    pad_ref[...] = jnp.zeros_like(pad_ref)
    pad_ref[8 : 8 + cells, :] = smeared
    total = slit_ref[0] * pad_ref[4 : 4 + cells, :]
    for tap in range(1, 9):
        total += slit_ref[tap] * pad_ref[4 + tap : 4 + tap + cells, :]
    out_ref[...] = total


def partial_image(pop, parts, starts, slit, outputs):
    cells = pop.shape[0]
    vmem = pl.BlockSpec(memory_space=pltpu.VMEM)
    return pl.pallas_call(
        functools.partial(image_kernel, starts=starts),
        out_shape=jax.ShapeDtypeStruct((cells, outputs + 128), F32),
        in_specs=[pl.BlockSpec(memory_space=pltpu.SMEM)] + [vmem] * (1 + len(parts)),
        scratch_shapes=[
            pltpu.VMEM((outputs + 2 * REACH, L), F32),
            pltpu.VMEM((cells + 16, outputs + 128), F32),
        ],
        compiler_params=pltpu.CompilerParams(vmem_limit_bytes=VMEM_LIMIT),
        cost_estimate=pl.CostEstimate(flops=4 * cells * L * (outputs + 128), bytes_accessed=cells * L * 2, transcendentals=0),
        name="image",
    )(slit, pop, *parts)


def swap(values, offset, count):
    return lax.ppermute(values, "blk", [(i, i ^ offset) for i in range(count)])


def gather_steps(count):
    steps = []
    offset = count
    while offset > 4:
        size = min(4, offset // 4)
        offset //= size
        steps.append([offset * i for i in range(1, size)])
    while offset > 1:
        offset //= 2
        steps.append([offset])
    return steps


def gathered_level(level, steps, own_levels):
    owner = (level // own_levels) ^ lax.axis_index("blk")
    position = jnp.zeros_like(level)
    blocks = 1
    for offsets in steps:
        size = len(offsets) + 1
        position += ((owner // offsets[0]) % size) * blocks
        blocks *= size
    return position * own_levels + level % own_levels


def body(pop_cells, cell_map, line_level, line_strength, inst_wave, inst_slit):
    count = lax.axis_size("blk")
    own_levels = pop_cells.shape[0]
    bins = line_level.shape[0] // LINES_BIN
    outputs, chunks = bins // BINS, bins // CHUNK
    cells = CELL_DEV * count
    steps = gather_steps(count)

    onehot = (cell_map[None, :] == jnp.arange(cells, dtype=jnp.int32)[:, None]).astype(BF16)
    pop = lax.dot_general(onehot, pop_cells, CONTRACT_LAST, preferred_element_type=F32).astype(BF16)

    level = gathered_level(line_level, steps, own_levels).reshape(-1, 128)
    strength = line_strength.reshape(-1, 128)
    wave = jnp.pad(inst_wave, (0, 512 - inst_wave.shape[0])).reshape(1, 512)
    part_steps = SPLIT
    parts, starts = [], []
    first = 0
    for index, offsets in enumerate(steps):
        pieces = [pop] + [swap(pop, k, count) for k in offsets]
        place = index - (len(steps) - 3)
        if place >= 0 and part_steps[place]:
            parts.append(blurred_emission(level, strength, wave, first, part_steps[place]))
            starts.append(first * (CHUNK // BINS))
            first += part_steps[place]
            pieces, parts[-1] = lax.optimization_barrier((pieces, parts[-1]))
        pop = jnp.concatenate(pieces, axis=1)
    wide = partial_image(pop, parts, starts, inst_slit, outputs)
    got = lax.all_to_all(wide, "blk", split_axis=0, concat_axis=0, tiled=True)
    got = got.reshape(count, CELL_DEV, outputs + 128)
    lane = jnp.arange(outputs)
    after = jnp.pad(jnp.where(lane < REACH, got[:-1, :, outputs:], 0), ((1, 0), (0, 0), (0, 0)))
    before = jnp.pad(jnp.where(lane >= outputs - REACH, got[1:, :, outputs:], 0), ((0, 1), (0, 0), (0, 0)))
    image = got[:, :, :outputs] + after + before
    return jnp.transpose(image, (1, 0, 2)).reshape(CELL_DEV, count * outputs)


def solution(mesh):
    placed = (P("blk", "groups"), P(), P("blk"), P("blk"), P(), P())
    return jax.shard_map(
        body, mesh=mesh, in_specs=placed, out_specs=P(("groups", "blk"), None), check_vma=False
    )
```

time: 256 us -> 42.7 us (0.17)
  other arithmetic: 191 us -> 2.18 us
  blocking collectives: 15.9 us -> 0 us
  matrix products: 16 us -> 0.91 us
  between operations: 13.8 us -> 0.13 us
  waiting for transfers between devices: 3.21 us -> 14.4 us
  starting transfers between devices: 3.73 us -> 13.4 us
  local copies, waits for them, and re-layouts: 12.2 us -> 2.57 us
  Pallas kernels: 0 us -> 8.79 us
    unnamed x4 -> x0, other arithmetic: 179 us -> none
    all_to_all x1 -> x0, blocking collectives: 15.9 us -> none  [body(): lax.all_to_all(blurred, 'blk', split_axis=0, concat_axis=1, tiled=True)]
    dot_general x19 -> x1, matrix products: 16 us -> 0.91 us  [body(): lax.dot_general(onehot, pop_cells, CONTRACT_LAST, preferred_element_type=...]
    all_to_all x0 -> x1, waiting for transfers between devices: none -> 10 us  [body(): got = lax.all_to_all(wide, 'blk', split_axis=0, concat_axis=0, tiled=True)]
    pallas_call x0 -> x3, Pallas kernels: none -> 8.79 us  [the longest x2 6.51 us: blurred_emission(): pl.pallas_call(functools.partial(emission_kernel, first_chunk=first_chunk...]
    convert_element_type x1 -> x0, local copies, waits for them, and re-layouts: 7.32 us -> none  [body(): emission_t = jnp.zeros((W_DEV, L), jnp.float32).at[line_bins, line_level]...]
    all_to_all x0 -> x1, starting transfers between devices: none -> 5.89 us  [body(): got = lax.all_to_all(wide, 'blk', split_axis=0, concat_axis=0, tiled=True)]
    add x2 -> x0, other arithmetic: 5.87 us -> none  [the longest x1 5.76 us: slit_blur(): total = total + inst_slit[tap_index] * padded[tap_index:tap_index + cells]]
  transfers between devices with their start and end apart: 3 -> 6, of which waited for: 1 -> 3; matrix products, arithmetic and copies ran while one was open for 75% -> 5% of each run, Pallas kernels for 0% -> 15%
where the time goes in v1:
time: 42.7 us; the launch traced here: 42.4 us
  waiting for transfers between devices  14.4 us (34%)
  starting transfers between devices  13.4 us (31%)
  Pallas kernels  8.79 us (21%)
  local copies, waits for them, and re-layouts  2.57 us (6%)
  other arithmetic  2.18 us (5%)
  matrix products  0.91 us (2%)
    all_to_all x1, waiting for transfers between devices, body(): got = lax.all_to_all(wide, 'blk', split_axis=0, concat_axis=0, tiled=True)  10 us
    ppermute x5, starting transfers between devices, swap(): return lax.ppermute(values, 'blk', [(i, i ^ offset) for i in range(count)])  7.56 us
    pallas_call x2, Pallas kernels, blurred_emission(): pl.pallas_call(functools.partial(emission_kernel, first_chunk=first_chunk...  6.51 us
    all_to_all x1, starting transfers between devices, body(): got = lax.all_to_all(wide, 'blk', split_axis=0, concat_axis=0, tiled=True)  5.89 us
    ppermute x5, waiting for transfers between devices, swap(): return lax.ppermute(values, 'blk', [(i, i ^ offset) for i in range(count)])  4.38 us
    pallas_call x1, Pallas kernels, partial_image(): pl.pallas_call(functools.partial(image_kernel, starts=starts), out_shape=...  2.28 us
    unnamed x9, local copies, waits for them, and re-layouts  1.87 us
    reshape x1, other arithmetic, body(): level = gathered_level(line_level, steps, own_levels).reshape(-1, 128)  1.31 us
  transfers between devices with their start and end apart: 6, of which 3 were waited for; matrix products, arithmetic and copies ran while one was open for 5% of the time, Pallas kernels for 15%

profile of v1, /device:TPU:0, one launch (start us, length us, event | category | flops | bytes accessed | tf_op | source)
XLA Modules:
  0.0 42.4 jit_solution(6066482859014843906)
XLA Ops:
  0.0 0.9 %copy-done = bf16[128,512]{1,0:T(8,128)(2,1)S(1)} copy-done((bf16[128,512]{1,0:T(8,128)(2,1)S(1)}, bf16[128,512]{1,0:T(8,128)(2,1)}, u32[]{:S(2)}) %copy-start) | copy-done | bytes 131096
  0.9 0.9 %convolution_convert_fusion = bf16[256,128]{1,0:T(8,128)(2,1)S(1)} fusion(bf16[128,512]{1,0:T(8,128)(2,1)S(1)} %copy-done, s32[512]{0:T(512)} %param.7), kind=kOutput, calls=%fused_computation | convolution fusion | flops 33718272 | bytes 198656 | tf_op jit(solution)/shard_map/dot_general | solution.py:184
  1.8 3.1 %collective-permute-start = (bf16[256,128]{1,0:T(8,128)(2,1)S(1)}, bf16[256,128]{1,0:T(8,128)(2,1)S(1)}, u32[]{:S(2)}, u32[]{:S(2)}) collective-permute-start(bf16[256,128]{1,0:T(8,128)(2,1)S(1)} %convolution_convert_fusion), channel_id=1, source_target_pairs={{0,4},{1,5},{2,6},{3,7},{4,0},{5,1},{6,2},{7,3},{8,12},{9,13},{10,... | collective-permute-start | bytes 196616 | tf_op jit(solution)/shard_map/ppermute | solution.py:148
  4.9 2.6 %collective-permute-start.1 = (bf16[256,128]{1,0:T(8,128)(2,1)S(1)}, bf16[256,128]{1,0:T(8,128)(2,1)S(1)}, u32[]{:S(2)}, u32[]{:S(2)}) collective-permute-start(bf16[256,128]{1,0:T(8,128)(2,1)S(1)} %convolution_convert_fusion), channel_id=1, source_target_pairs={{0,8},{1,9},{2,10},{3,11},{4,12},{5,13},{6,14},{7,15},{8,0},{9,1},... | collective-permute-start | bytes 196616 | tf_op jit(solution)/shard_map/ppermute | solution.py:148
  7.5 0.0 collective-permute-start.2
  7.5 1.3 %fusion.8.level_ref = s32[256,128]{1,0:T(8,128)S(1)} fusion(s32[32768]{0:T(1024)} %param.8, s32[]{:T(128)S(6)} %axis_index.12), kind=kLoop, calls=%fused_computation.31 | loop fusion | flops 2523136 | bytes 262148 | tf_op jit(solution)/shard_map/reshape | solution.py:186
  8.8 0.7 %pad.12 = f32[512]{0:T(512)S(1)} pad(f32[129]{0:T(256)} %param.10, f32[]{:T(128)} %constant.91.clone.1), padding=0_383 | pad | bytes 2568 | tf_op jit(solution)/shard_map/jit(_pad)/pad | solution.py:188
  9.5 0.9 %copy-done.2 = f32[32768]{0:T(1024)S(1)} copy-done((f32[32768]{0:T(1024)S(1)}, f32[32768]{0:T(1024)}, u32[]{:S(2)}) %copy-start.2) | copy-done | bytes 131096
  10.4 3.3 %emission.2.refs_0_ = f32[80,2048]{1,0:T(8,128)S(1)} custom-call(s32[256,128]{1,0:T(8,128)S(1)} %fusion.8.level_ref, f32[256,128]{1,0:T(8,128)S(1)} %bitcast.14, f32[1,512]{1,0:T(1,128)S(1)} %bitcast.12), custom_call_target="tpu_custom_call" | custom-call | flops 469762048 | bytes 131072 | tf_op jit(solution)/shard_map/emission/pallas_call | solution.py:92
  13.7 0.0 collective-permute-done
  13.7 0.0 collective-permute-done.1
  13.7 0.0 collective-permute-done.2
  13.8 1.8 %collective-permute-start.3 = (bf16[256,512]{1,0:T(8,128)(2,1)S(1)}, bf16[256,512]{1,0:T(8,128)(2,1)S(1)}, u32[]{:S(2)}, u32[]{:S(2)}) collective-permute-start(bf16[256,512]{1,0:T(8,128)(2,1)S(1)} %constant_dynamic-update-slice_fusion), channel_id=1, source_target_pairs={{0,2},{1,3},{2,0},{3,1},{4,6},{5,7},{6,4},{7,5},{8,10},{9,11},{10,... | collective-permute-start | bytes 786440 | tf_op jit(solution)/shard_map/ppermute | solution.py:148
  15.6 3.3 %emission.3.refs_1_ = f32[80,2048]{1,0:T(8,128)S(1)} custom-call(s32[256,128]{1,0:T(8,128)S(1)} %fusion.8.level_ref, f32[256,128]{1,0:T(8,128)S(1)} %bitcast.15, f32[1,512]{1,0:T(1,128)S(1)} %bitcast.13), custom_call_target="tpu_custom_call" | custom-call | flops 469762048 | bytes 131072 | tf_op jit(solution)/shard_map/emission/pallas_call | solution.py:92
  18.9 2.5 %collective-permute-done.3 = bf16[256,512]{1,0:T(8,128)(2,1)S(1)} collective-permute-done((bf16[256,512]{1,0:T(8,128)(2,1)S(1)}, bf16[256,512]{1,0:T(8,128)(2,1)S(1)}, u32[]{:S(2)}, u32[]{:S(2)}) %collective-permute-start.3) | collective-permute-done | bytes 262176 | tf_op jit(solution)/shard_map/ppermute | solution.py:148
  21.3 0.1 pad_maximum_fusion.1
  21.4 0.0 copy-start.1
  21.4 0.1 collective-permute-start.4
  21.5 1.9 %collective-permute-done.4 = bf16[256,1024]{1,0:T(8,128)(2,1)S(1)} collective-permute-done((bf16[256,1024]{1,0:T(8,128)(2,1)S(1)}, bf16[256,1024]{1,0:T(8,128)(2,1)S(1)}, u32[]{:S(2)}, u32[]{:S(2)}) %collective-permute-start.4) | collective-permute-done | bytes 524320 | tf_op jit(solution)/shard_map/ppermute | solution.py:148
  23.4 0.1 pad_maximum_fusion.pop_ref
  23.5 2.3 %image.1 = f32[256,256]{1,0:T(8,128)} custom-call(f32[9]{0:T(128)S(1)} %copy-done.1, bf16[256,2048]{1,0:T(8,128)(2,1)S(1)} %pad_maximum_fusion.pop_ref, f32[80,2048]{1,0:T(8,128)S(1)} %emission.2.refs_0_, f32[80,2048]{1,0:T(8,128)S(1)} %emission.3.refs_1_), custom_call_target="tpu_custom_call" | custom-call | flops 536870912 | bytes 1048576 | tf_op jit(solution)/shard_map/image/pallas_call | solution.py:133
  25.8 5.9 %all-to-all-start = ((f32[16,16,256]{2,1,0:T(8,128)}), f32[16,16,256]{2,1,0:T(8,128)S(1)}, u32[]{:S(2)}, u32[]{:S(2)}) async-start(f32[16,16,256]{2,1,0:T(8,128)} %bitcast.3), calls=%async_computation | async-start | bytes 524288 | tf_op jit(solution)/shard_map/all_to_all | solution.py:202
  31.7 10.0 %all-to-all-done = f32[16,16,256]{2,1,0:T(8,128)S(1)} async-done(((f32[16,16,256]{2,1,0:T(8,128)}), f32[16,16,256]{2,1,0:T(8,128)S(1)}, u32[]{:S(2)}, u32[]{:S(2)}) %all-to-all-start) | async-done | bytes 262176 | tf_op jit(solution)/shard_map/all_to_all | solution.py:202
  41.8 0.7 %copy_bitcast_fusion = f32[16,2048]{1,0:T(8,128)} fusion(f32[16,16,256]{2,1,0:T(8,128)S(1)} %all-to-all-done, f32[15,16,128]{2,1,0:T(8,128)S(1)} %get-tuple-element.22, f32[15,16,128]{2,1,0:T(8,128)S(1)} %get-tuple-element.21), kind=kLoop, calls=%fused_computation.35 | loop fusion | flops 65536 | bytes 507904 | tf_op jit(solution)/shard_map/reshape | solution.py:208
  (9 shorter events, 0.1 us)
Async XLA Ops:
  0.0 0.9 %copy-start = (bf16[128,512]{1,0:T(8,128)(2,1)S(1)}, bf16[128,512]{1,0:T(8,128)(2,1)}, u32[]{:S(2)}) copy-start(bf16[128,512]{1,0:T(8,128)(2,1)} %param.6) | copy-start | bytes 393220
  1.8 11.8 %collective-permute-start = (bf16[256,128]{1,0:T(8,128)(2,1)S(1)}, bf16[256,128]{1,0:T(8,128)(2,1)S(1)}, u32[]{:S(2)}, u32[]{:S(2)}) collective-permute-start(bf16[256,128]{1,0:T(8,128)(2,1)S(1)} %convolution_convert_fusion), channel_id=1, source_target_pairs={{0,4},{1,5},{2,6},{3,7},{4,0},{5,1},{6,2},{7,3},{8,12},{9,13},{10,... | collective-permute-start | bytes 196616 | tf_op jit(solution)/shard_map/ppermute | solution.py:148
  4.9 8.8 %collective-permute-start.1 = (bf16[256,128]{1,0:T(8,128)(2,1)S(1)}, bf16[256,128]{1,0:T(8,128)(2,1)S(1)}, u32[]{:S(2)}, u32[]{:S(2)}) collective-permute-start(bf16[256,128]{1,0:T(8,128)(2,1)S(1)} %convolution_convert_fusion), channel_id=1, source_target_pairs={{0,8},{1,9},{2,10},{3,11},{4,12},{5,13},{6,14},{7,15},{8,0},{9,1},... | collective-permute-start | bytes 196616 | tf_op jit(solution)/shard_map/ppermute | solution.py:148
  7.5 6.2 %collective-permute-start.2 = (bf16[256,128]{1,0:T(8,128)(2,1)S(1)}, bf16[256,128]{1,0:T(8,128)(2,1)S(1)}, u32[]{:S(2)}, u32[]{:S(2)}) collective-permute-start(bf16[256,128]{1,0:T(8,128)(2,1)S(1)} %convolution_convert_fusion), channel_id=1, source_target_pairs={{0,12},{1,13},{2,14},{3,15},{4,8},{5,9},{6,10},{7,11},{8,4},{9,5},... | collective-permute-start | bytes 196616 | tf_op jit(solution)/shard_map/ppermute | solution.py:148
  9.5 0.9 %copy-start.2 = (f32[32768]{0:T(1024)S(1)}, f32[32768]{0:T(1024)}, u32[]{:S(2)}) copy-start(f32[32768]{0:T(1024)} %param.9) | copy-start | bytes 393220
  13.8 7.5 %collective-permute-start.3 = (bf16[256,512]{1,0:T(8,128)(2,1)S(1)}, bf16[256,512]{1,0:T(8,128)(2,1)S(1)}, u32[]{:S(2)}, u32[]{:S(2)}) collective-permute-start(bf16[256,512]{1,0:T(8,128)(2,1)S(1)} %constant_dynamic-update-slice_fusion), channel_id=1, source_target_pairs={{0,2},{1,3},{2,0},{3,1},{4,6},{5,7},{6,4},{7,5},{8,10},{9,11},{10,... | collective-permute-start | bytes 786440 | tf_op jit(solution)/shard_map/ppermute | solution.py:148
  21.4 2.1 %copy-start.1 = (f32[9]{0:T(128)S(1)}, f32[9]{0:T(128)}, u32[]{:S(2)}) copy-start(f32[9]{0:T(128)} %slit_ref.1) | copy-start | bytes 112
  21.4 2.0 %collective-permute-start.4 = (bf16[256,1024]{1,0:T(8,128)(2,1)S(1)}, bf16[256,1024]{1,0:T(8,128)(2,1)S(1)}, u32[]{:S(2)}, u32[]{:S(2)}) collective-permute-start(bf16[256,1024]{1,0:T(8,128)(2,1)S(1)} %pad_maximum_fusion.1), channel_id=1, source_target_pairs={{0,1},{1,0},{2,3},{3,2},{4,5},{5,4},{6,7},{7,6},{8,9},{9,8},{10,11... | collective-permute-start | bytes 1572872 | tf_op jit(solution)/shard_map/ppermute | solution.py:148
  25.8 15.9 %all-to-all-start = ((f32[16,16,256]{2,1,0:T(8,128)}), f32[16,16,256]{2,1,0:T(8,128)S(1)}, u32[]{:S(2)}, u32[]{:S(2)}) async-start(f32[16,16,256]{2,1,0:T(8,128)} %bitcast.3), calls=%async_computation | async-start | bytes 524288 | tf_op jit(solution)/shard_map/all_to_all | solution.py:202

commit v2 on v0

v2 whole, which is shorter than its diff:
```python
import functools

import jax
import jax.numpy as jnp
from jax import lax
from jax.experimental import pallas as pl
from jax.experimental.pallas import tpu as pltpu
from jax.sharding import PartitionSpec as P

L = 2048
LINES_BIN = 32
CELL_DEV = 16
LOW = 128
HIGH = L // LOW
BINS = 8
CHUNK = 256
REACH = 8
CHUNK_OUT = CHUNK // BINS
SPAN = CHUNK_OUT + 2 * REACH
CHUNK_ROWS = CHUNK * LINES_BIN // 128
TAP_WIDTH = 512
UNROLL = 4
BF16 = jnp.bfloat16
F32 = jnp.float32
VMEM_LIMIT = 48 * 1024 * 1024
CONTRACT_LAST = (((1,), (1,)), ((), ()))
VMEM = pl.BlockSpec(memory_space=pltpu.VMEM)
SMEM = pl.BlockSpec(memory_space=pltpu.SMEM)


def two_terms(values):
    first = values.astype(BF16)
    return first, (values - first.astype(F32)).astype(BF16)


def tap_matrix(wave_ref, tap_ref):
    tap_ref[...] = jnp.zeros_like(tap_ref)
    tap_ref[:, : wave_ref.shape[1]] = jnp.broadcast_to(wave_ref[...], (8, wave_ref.shape[1]))
    base = jnp.concatenate([tap_ref[...]] * (SPAN // 8), axis=0)
    taps = pltpu.roll(base, TAP_WIDTH - 128, 1, stride=BINS, stride_axis=0)[:, :CHUNK]
    return taps


def emission(lines, own_levels, scratch):
    level_ref, strength_ref, first_row, rows = lines
    high_ref, low_ref, em_ref = scratch
    level = level_ref[first_row : first_row + rows, :].astype(jnp.int32)
    owner = level // own_levels
    row_bin = lax.broadcasted_iota(jnp.int32, (rows, 128), 0) % 2 * (128 // LINES_BIN)
    lane_bin = lax.broadcasted_iota(jnp.int32, (rows, 128), 1) // LINES_BIN
    high_ref[:rows, :] = (owner % HIGH * BINS + row_bin + lane_bin).astype(F32)
    low_ref[:rows, :] = (owner // HIGH * own_levels + level % own_levels).astype(F32)

    choices = [
        (lax.broadcasted_iota(jnp.int32, (16, 128), 0) + 16 * block).astype(F32).astype(BF16)
        for block in range(LOW // 16)
    ]
    zero = jnp.zeros((16, 128), BF16)
    one = jnp.ones((16, 128), BF16)

    def spread(ref, index):
        return jnp.broadcast_to(ref[pl.ds(index, 1), :], (16, 128)).astype(BF16)

    def half(index):
        high = spread(high_ref, index)
        low = spread(low_ref, index)
        strength = spread(strength_ref, first_row + index)
        a = jnp.concatenate([jnp.where(high == choice, strength, zero) for choice in choices], axis=0)
        b = jnp.concatenate([jnp.where(low == choice, one, zero) for choice in choices], axis=0)
        return a, b

    def group(index):
        a0, b0 = half(2 * index)
        a1, b1 = half(2 * index + 1)
        return lax.dot_general(
            jnp.concatenate([a0, a1], axis=1),
            jnp.concatenate([b0, b1], axis=1),
            CONTRACT_LAST,
            preferred_element_type=F32,
        )

    @pl.loop(0, rows // 4, unroll=UNROLL)
    def _(pair):
        x = group(2 * pair)
        y = group(2 * pair + 1)
        place = pl.ds(pl.multiple_of(16 * pair, 16), 16)
        for h in range(HIGH):
            own = slice(BINS * h, BINS * h + BINS)
            em_ref[place, h * LOW : (h + 1) * LOW] = jnp.concatenate([x[own], y[own]], axis=0).astype(BF16)


def blurred(taps, em):
    rows = taps.shape[0]
    both = jnp.dot(jnp.concatenate(two_terms(taps), axis=0), em, preferred_element_type=F32)
    return both[:rows] + both[rows:]


def add_chunks(total_ref, chunks, taps, level_ref, strength_ref, own_levels, scratch):
    for chunk in chunks:
        emission((level_ref, strength_ref, chunk * CHUNK_ROWS, CHUNK_ROWS), own_levels, scratch)
        place = slice(chunk * CHUNK_OUT, chunk * CHUNK_OUT + SPAN)
        total_ref[place, :] += blurred(taps, scratch[-1][...])


def first_kernel(level_ref, strength_ref, wave_ref, total_ref, tap_ref, *scratch, chunks, own_levels):
    total_ref[...] = jnp.zeros_like(total_ref)
    taps = tap_matrix(wave_ref, tap_ref)
    add_chunks(total_ref, chunks, taps, level_ref, strength_ref, own_levels, scratch)


def last_kernel(
    level_ref, strength_ref, wave_ref, given_ref, out_ref, total_ref, tap_ref, *scratch, chunks, own_levels
):
    outputs = total_ref.shape[0] - 2 * REACH
    total_ref[...] = given_ref[...]
    taps = tap_matrix(wave_ref, tap_ref)
    add_chunks(total_ref, chunks, taps, level_ref, strength_ref, own_levels, scratch)
    first, second = two_terms(total_ref[REACH : REACH + outputs, :])
    out_ref[:outputs, :] = first
    out_ref[outputs : 2 * outputs, :] = second
    edges = jnp.concatenate([total_ref[REACH + outputs :, :], total_ref[:REACH, :]], axis=0)
    first, second = two_terms(edges)
    out_ref[2 * outputs : 2 * outputs + 2 * REACH, :] = first
    out_ref[2 * outputs + 2 * REACH :, :] = second


def emission_call(kernel, out_shape, operands, chunks, extra=()):
    scratch = [
        pltpu.VMEM((8, TAP_WIDTH), F32),
        pltpu.VMEM((CHUNK_ROWS, 128), F32),
        pltpu.VMEM((CHUNK_ROWS, 128), F32),
        pltpu.VMEM((CHUNK, L), BF16),
    ]
    return pl.pallas_call(
        kernel,
        out_shape=out_shape,
        in_specs=[VMEM] * len(operands),
        scratch_shapes=list(extra) + scratch,
        compiler_params=pltpu.CompilerParams(vmem_limit_bytes=VMEM_LIMIT),
        cost_estimate=pl.CostEstimate(
            flops=2 * chunks * CHUNK * L * 1024, bytes_accessed=chunks * CHUNK * 256, transcendentals=0
        ),
        name="emission",
    )(*operands)


def products(total, terms_ref, pop_refs, offsets):
    me = lax.axis_index("blk") % HIGH

    def block(offset):
        return terms_ref[:, pl.ds(pl.multiple_of((me ^ offset) * LOW, LOW), LOW)]

    for pop_ref, own in zip(pop_refs, offsets):
        for i in range(0, len(own), 2):
            terms = jnp.concatenate([block(own[i]), block(own[i + 1])], axis=1)
            pop = pop_ref[:, i * LOW : (i + 2) * LOW]
            new = lax.dot_general(pop, terms, CONTRACT_LAST, preferred_element_type=F32)
            total = new if total is None else total + new
    return total


def early_kernel(terms_ref, *refs, offsets):
    refs[-1][...] = products(None, terms_ref, refs[:-1], offsets)


def image_kernel(slit_ref, terms_ref, given_ref, *refs, offsets):
    pop_refs, (out_ref, pad_ref) = refs[:-2], refs[-2:]
    cells, outputs = pop_refs[0].shape[0], out_ref.shape[2]
    total = products(given_ref[...], terms_ref, pop_refs, offsets)
    edge = 2 * REACH
    pad_ref[:8, :] = jnp.zeros((8, pad_ref.shape[1]), F32)
    pad_ref[8 + cells :, :] = jnp.zeros((8, pad_ref.shape[1]), F32)
    pad_ref[8 : 8 + cells, :outputs] = total[:, :outputs] + total[:, outputs : 2 * outputs]
    pad_ref[8 : 8 + cells, outputs : outputs + edge] = (
        total[:, 2 * outputs : 2 * outputs + edge] + total[:, 2 * outputs + edge :]
    )
    image = slit_ref[0] * pad_ref[4 : 4 + cells, :]
    for tap in range(1, 9):
        image += slit_ref[tap] * pad_ref[4 + tap : 4 + tap + cells, :]
    lane = lax.broadcasted_iota(jnp.int32, (8, 128), 1)
    for place in range(cells // CELL_DEV):
        own = image[place * CELL_DEV : (place + 1) * CELL_DEV]
        out_ref[place, :CELL_DEV, :] = own[:, :outputs]
        moved = pltpu.roll(own[8:, outputs:], edge, 1)
        out_ref[place, CELL_DEV:, :] = jnp.where(lane < edge, own[:8, outputs:], moved)


def join(got):
    count, outputs = got.shape[0], got.shape[2]
    edge = got[:, CELL_DEV:, :]
    after = jnp.concatenate([edge[:-1, :, :REACH], edge[:-1, :, 2 * REACH : 3 * REACH]], axis=1)
    before = jnp.concatenate([edge[1:, :, REACH : 2 * REACH], edge[1:, :, 3 * REACH : 4 * REACH]], axis=1)
    image = got[:, :CELL_DEV, :]
    image += jnp.pad(after, ((1, 0), (0, 0), (0, outputs - REACH)))
    image += jnp.pad(before, ((0, 1), (0, 0), (outputs - REACH, 0)))
    return jnp.transpose(image, (1, 0, 2)).reshape(CELL_DEV, count * outputs)


def early_products(terms, pops, offsets):
    return pl.pallas_call(
        functools.partial(early_kernel, offsets=offsets),
        out_shape=jax.ShapeDtypeStruct((pops[0].shape[0], terms.shape[0]), F32),
        in_specs=[VMEM] * (1 + len(pops)),
        compiler_params=pltpu.CompilerParams(vmem_limit_bytes=VMEM_LIMIT),
        cost_estimate=pl.CostEstimate(flops=3 << 28, bytes_accessed=1 << 20, transcendentals=0),
        name="early",
    )(terms, *pops)


def slit_image(slit, terms, given, pops, offsets):
    cells, outputs = pops[0].shape[0], terms.shape[0] // 2 - 2 * REACH
    return pl.pallas_call(
        functools.partial(image_kernel, offsets=offsets),
        out_shape=jax.ShapeDtypeStruct((cells // CELL_DEV, CELL_DEV + 8, outputs), F32),
        in_specs=[SMEM] + [VMEM] * (2 + len(pops)),
        scratch_shapes=[pltpu.VMEM((cells + 16, outputs + 128), F32)],
        compiler_params=pltpu.CompilerParams(vmem_limit_bytes=VMEM_LIMIT),
        cost_estimate=pl.CostEstimate(flops=1 << 28, bytes_accessed=1 << 20, transcendentals=0),
        name="image",
    )(slit, terms, given, *pops)


def swap(values, offset, count):
    return lax.ppermute(values, "blk", [(i, i ^ offset) for i in range(count)])


def body(pop_cells, cell_map, line_level, line_strength, inst_wave, inst_slit):
    count = lax.axis_size("blk")
    own_levels = pop_cells.shape[0]
    bins = line_level.shape[0] // LINES_BIN
    outputs, chunks = bins // BINS, bins // CHUNK
    cells = CELL_DEV * count
    hold = lax.optimization_barrier

    onehot = (cell_map[None, :] == jnp.arange(cells, dtype=jnp.int32)[:, None]).astype(BF16)
    pop = lax.dot_general(onehot, pop_cells, CONTRACT_LAST, preferred_element_type=F32).astype(BF16)
    if count > HIGH:
        sets = [list(range(i, count, HIGH)) for i in range(HIGH)]
        pop = lax.all_gather(pop, "blk", axis=1, tiled=True, axis_index_groups=sets)

    lines = (line_level.reshape(-1, 128), line_strength.reshape(-1, 128), inst_wave.reshape(1, -1))
    far = [swap(pop, k, count) for k in (4, 8, 12)]
    total = emission_call(
        functools.partial(first_kernel, chunks=range(chunks // 2), own_levels=own_levels),
        jax.ShapeDtypeStruct((outputs + 2 * REACH, L), F32),
        lines,
        chunks // 2,
    )
    far, total = hold((far, total))
    line = jnp.concatenate([pop] + list(far), axis=1)
    across = swap(line, 2, count)
    line_pair = swap(line, 1, count)
    terms = emission_call(
        functools.partial(last_kernel, chunks=range(chunks // 2, chunks), own_levels=own_levels),
        jax.ShapeDtypeStruct((2 * outputs + 4 * REACH, L), BF16),
        lines + (total,),
        chunks - chunks // 2,
        [pltpu.VMEM((outputs + 2 * REACH, L), F32)],
    )
    across, terms = hold((across, terms))
    across_pair = swap(across, 1, count)
    offsets = [[k ^ offset for k in (0, 4, 8, 12)] for offset in (0, 1, 2, 3)]
    early = early_products(terms, [line, line_pair, across], offsets[:3])
    across_pair, early = hold((across_pair, early))
    image = slit_image(inst_slit, terms, early, [across_pair], offsets[3:])
    return join(lax.all_to_all(image, "blk", split_axis=0, concat_axis=0, tiled=True))


def solution(mesh):
    placed = (P("blk", "groups"), P(), P("blk"), P("blk"), P(), P())
    return jax.shard_map(
        body, mesh=mesh, in_specs=placed, out_specs=P(("groups", "blk"), None), check_vma=False
    )
```

time: 256 us -> 39.4 us (0.15)
  other arithmetic: 191 us -> 0.8 us
  matrix products: 16 us -> 0.91 us
  between operations: 13.8 us -> 0.07 us
  local copies, waits for them, and re-layouts: 12.2 us -> 3.5 us
  Pallas kernels: 0 us -> 8.27 us
  starting transfers between devices: 3.73 us -> 7.27 us
    unnamed x4 -> x0, other arithmetic: 179 us -> none
    dot_general x19 -> x1, matrix products: 16 us -> 0.91 us  [body(): lax.dot_general(onehot, pop_cells, CONTRACT_LAST, preferred_element_type=...]
    pallas_call x0 -> x4, Pallas kernels: none -> 8.27 us  [the longest x2 6.52 us: emission_call(): pl.pallas_call(kernel, out_shape=out_shape, in_specs=[VMEM] * len(operand...]
    convert_element_type x1 -> x0, local copies, waits for them, and re-layouts: 7.32 us -> none  [body(): emission_t = jnp.zeros((W_DEV, L), jnp.float32).at[line_bins, line_level]...]
    add x2 -> x0, other arithmetic: 5.87 us -> none  [the longest x1 5.76 us: slit_blur(): total = total + inst_slit[tap_index] * padded[tap_index:tap_index + cells]]
    convert_element_type x1 -> x0, other arithmetic: 5.09 us -> none  [body(): emission_t = jnp.zeros((W_DEV, L), jnp.float32).at[line_bins, line_level]...]
    ppermute x2 -> x6, starting transfers between devices: 3.73 us -> 7.27 us  [swap(): return lax.ppermute(values, 'blk', [(i, i ^ offset) for i in range(count)])]
  transfers between devices with their start and end apart: 3 -> 6, of which waited for: 1 -> 3; matrix products, arithmetic and copies ran while one was open for 75% -> 0% of each run, Pallas kernels for 0% -> 18%
where the time goes in v2:
time: 39.4 us; the launch traced here: 39.1 us
  blocking collectives  14.7 us (37%)
  Pallas kernels  8.27 us (21%)
  starting transfers between devices  7.27 us (18%)
  waiting for transfers between devices  3.62 us (9%)
  local copies, waits for them, and re-layouts  3.5 us (9%)
  matrix products  0.91 us (2%)
  other arithmetic  0.8 us (2%)
    all_to_all x1, blocking collectives, body(): lax.all_to_all(image, 'blk', split_axis=0, concat_axis=0, tiled=True)  14.7 us
    ppermute x6, starting transfers between devices, swap(): return lax.ppermute(values, 'blk', [(i, i ^ offset) for i in range(count)])  7.27 us
    pallas_call x2, Pallas kernels, emission_call(): pl.pallas_call(kernel, out_shape=out_shape, in_specs=[VMEM] * len(operand...  6.52 us
    ppermute x6, waiting for transfers between devices, swap(): return lax.ppermute(values, 'blk', [(i, i ^ offset) for i in range(count)])  3.62 us
    unnamed x10, local copies, waits for them, and re-layouts  3.4 us
    pallas_call x1, Pallas kernels, slit_image(): pl.pallas_call(functools.partial(image_kernel, offsets=offsets), out_shap...  1.19 us
    dot_general x1, matrix products, body(): lax.dot_general(onehot, pop_cells, CONTRACT_LAST, preferred_element_type=...  0.91 us
  transfers between devices with their start and end apart: 6, of which 3 were waited for; matrix products, arithmetic and copies ran while one was open for 0% of the time, Pallas kernels for 18%

profile of v2, /device:TPU:0, one launch (start us, length us, event | category | flops | bytes accessed | tf_op | source)
XLA Modules:
  0.0 39.1 jit_solution(4954111773244577230)
XLA Ops:
  0.0 0.9 %copy-done = bf16[128,512]{1,0:T(8,128)(2,1)S(1)} copy-done((bf16[128,512]{1,0:T(8,128)(2,1)S(1)}, bf16[128,512]{1,0:T(8,128)(2,1)}, u32[]{:S(2)}) %copy-start) | copy-done | bytes 131096
  0.9 0.9 %convolution_convert_fusion = bf16[256,128]{1,0:T(8,128)(2,1)S(1)} fusion(bf16[128,512]{1,0:T(8,128)(2,1)S(1)} %copy-done, s32[512]{0:T(512)} %param.7), kind=kOutput, calls=%fused_computation | convolution fusion | flops 33718272 | bytes 198656 | tf_op jit(solution)/shard_map/dot_general | solution.py:236
  1.8 3.1 %collective-permute-start = (bf16[256,128]{1,0:T(8,128)(2,1)S(1)}, bf16[256,128]{1,0:T(8,128)(2,1)S(1)}, u32[]{:S(2)}, u32[]{:S(2)}) collective-permute-start(bf16[256,128]{1,0:T(8,128)(2,1)S(1)} %convolution_convert_fusion), channel_id=1, source_target_pairs={{0,4},{1,5},{2,6},{3,7},{4,0},{5,1},{6,2},{7,3},{8,12},{9,13},{10,... | collective-permute-start | bytes 196616 | tf_op jit(solution)/shard_map/ppermute | solution.py:224
  4.9 2.6 %collective-permute-start.1 = (bf16[256,128]{1,0:T(8,128)(2,1)S(1)}, bf16[256,128]{1,0:T(8,128)(2,1)S(1)}, u32[]{:S(2)}, u32[]{:S(2)}) collective-permute-start(bf16[256,128]{1,0:T(8,128)(2,1)S(1)} %convolution_convert_fusion), channel_id=1, source_target_pairs={{0,8},{1,9},{2,10},{3,11},{4,12},{5,13},{6,14},{7,15},{8,0},{9,1},... | collective-permute-start | bytes 196616 | tf_op jit(solution)/shard_map/ppermute | solution.py:224
  7.5 0.0 collective-permute-start.2
  7.5 0.9 %copy-done.2 = s32[32768]{0:T(1024)S(1)} copy-done((s32[32768]{0:T(1024)S(1)}, s32[32768]{0:T(1024)}, u32[]{:S(2)}) %copy-start.2) | copy-done | bytes 131096
  8.4 0.9 %copy-done.3 = f32[32768]{0:T(1024)S(1)} copy-done((f32[32768]{0:T(1024)S(1)}, f32[32768]{0:T(1024)}, u32[]{:S(2)}) %copy-start.3) | copy-done | bytes 131096
  9.3 0.7 %copy-done.4 = f32[129]{0:T(256)S(1)} copy-done((f32[129]{0:T(256)S(1)}, f32[129]{0:T(256)}, u32[]{:S(2)}) %copy-start.4) | copy-done | bytes 540
  10.0 3.2 %emission.2.given_ref = f32[144,2048]{1,0:T(8,128)S(1)} custom-call(s32[256,128]{1,0:T(8,128)S(1)} %bitcast.10, f32[256,128]{1,0:T(8,128)S(1)} %bitcast.12, f32[1,129]{1,0:T(1,128)S(1)} %bitcast.14), custom_call_target="tpu_custom_call" | custom-call | flops 2147483648 | bytes 131072 | tf_op jit(solution)/shard_map/emission/pallas_call | solution.py:134
  13.2 0.0 collective-permute-done.1
  13.2 0.3 collective-permute-done.2
  13.6 1.6 %collective-permute-start.3 = (bf16[256,512]{1,0:T(8,128)(2,1)S(1)}, bf16[256,512]{1,0:T(8,128)(2,1)S(1)}, u32[]{:S(2)}, u32[]{:S(2)}) collective-permute-start(bf16[256,512]{1,0:T(8,128)(2,1)S(1)} %pad_maximum_fusion.refs_0_), channel_id=1, source_target_pairs={{0,2},{1,3},{2,0},{3,1},{4,6},{5,7},{6,4},{7,5},{8,10},{9,11},{10,... | collective-permute-start | bytes 786440 | tf_op jit(solution)/shard_map/ppermute | solution.py:224
  15.2 0.0 collective-permute-start.5
  15.2 3.3 %emission.3.terms_ref = bf16[288,2048]{1,0:T(8,128)(2,1)S(1)} custom-call(s32[256,128]{1,0:T(8,128)S(1)} %bitcast.11, f32[256,128]{1,0:T(8,128)S(1)} %bitcast.13, f32[1,129]{1,0:T(1,128)S(1)} %bitcast.15, f32[144,2048]{1,0:T(8,128)S(1)} %emission.2.given_ref), custom_call_target="tpu_custom_call" | custom-call | flops 2147483648 | bytes 131072 | tf_op jit(solution)/shard_map/emission/pallas_call | solution.py:134
  18.5 0.0 copy-start.1
  18.5 2.3 %collective-permute-done.3.refs_2_ = bf16[256,512]{1,0:T(8,128)(2,1)S(1)} collective-permute-done((bf16[256,512]{1,0:T(8,128)(2,1)S(1)}, bf16[256,512]{1,0:T(8,128)(2,1)S(1)}, u32[]{:S(2)}, u32[]{:S(2)}) %collective-permute-start.3) | collective-permute-done | bytes 262176 | tf_op jit(solution)/shard_map/ppermute | solution.py:224
  20.8 0.0 collective-permute-start.4
  20.8 0.0 collective-permute-done.5.refs_1_
  20.8 0.6 %early.1.given_ref = f32[256,288]{1,0:T(8,128)S(1)} custom-call(bf16[288,2048]{1,0:T(8,128)(2,1)S(1)} %emission.3.terms_ref, bf16[256,512]{1,0:T(8,128)(2,1)S(1)} %pad_maximum_fusion.refs_0_, bf16[256,512]{1,0:T(8,128)(2,1)S(1)} %collective-permute-done.5.refs_1_, bf16[256,512]{1,0:T(8,128)(2,1)S(1)} %collective-permute-done.3.refs_2_), custom_call_target="tpu_custom_call" | custom-call | flops 805306368 | bytes 1048576 | tf_op jit(solution)/shard_map/early/pallas_call | solution.py:200
  21.4 1.0 %collective-permute-done.4.refs_0_ = bf16[256,512]{1,0:T(8,128)(2,1)S(1)} collective-permute-done((bf16[256,512]{1,0:T(8,128)(2,1)S(1)}, bf16[256,512]{1,0:T(8,128)(2,1)S(1)}, u32[]{:S(2)}, u32[]{:S(2)}) %collective-permute-start.4) | collective-permute-done | bytes 262176 | tf_op jit(solution)/shard_map/ppermute | solution.py:224
  22.4 1.2 %image.1 = f32[16,24,128]{2,1,0:T(8,128)S(1)} custom-call(f32[9]{0:T(128)S(1)} %copy-done.1, bf16[288,2048]{1,0:T(8,128)(2,1)S(1)} %emission.3.terms_ref, f32[256,288]{1,0:T(8,128)S(1)} %early.1.given_ref, bf16[256,512]{1,0:T(8,128)(2,1)S(1)} %collective-permute-done.4.refs_0_), custom_call_target="tpu_custom_call" | custom-call | flops 268435456 | bytes 1048576 | tf_op jit(solution)/shard_map/image/pallas_call | solution.py:212
  23.6 14.7 %all_to_all.5 = f32[16,24,128]{2,1,0:T(8,128)S(1)} all-to-all(f32[16,24,128]{2,1,0:T(8,128)S(1)} %image.1), channel_id=1, replica_groups=mesh['groups'=2,'blk'=16] {'blk'}, dimensions={0} | all-to-all | bytes 393216 | tf_op jit(solution)/shard_map/all_to_all | solution.py:266
  38.2 0.1 fusion.4
  38.3 0.8 %copy_bitcast_fusion = f32[16,2048]{1,0:T(8,128)} fusion(f32[15,8,8]{2,1,0:T(8,128)S(1)} %get-tuple-element.22, f32[15,8,8]{2,1,0:T(8,128)S(1)} %get-tuple-element.23, f32[15,8,8]{2,1,0:T(8,128)S(1)} %get-tuple-element.24, f32[15,8,8]{2,1,0:T(8,128)S(1)} %get-tuple-element.21, f32[16,24,128]{2,1,0:T(8,128)S(1)} %all_to_all.5), kind=kLoop, calls=%fused_computation.4 | loop fusion | flops 589824 | bytes 507904 | tf_op jit(solution)/shard_map/reshape | solution.py:196
  (7 shorter events, 0.0 us)
Async XLA Ops:
  0.0 0.9 %copy-start = (bf16[128,512]{1,0:T(8,128)(2,1)S(1)}, bf16[128,512]{1,0:T(8,128)(2,1)}, u32[]{:S(2)}) copy-start(bf16[128,512]{1,0:T(8,128)(2,1)} %param.6) | copy-start | bytes 393220
  1.8 11.4 %collective-permute-start = (bf16[256,128]{1,0:T(8,128)(2,1)S(1)}, bf16[256,128]{1,0:T(8,128)(2,1)S(1)}, u32[]{:S(2)}, u32[]{:S(2)}) collective-permute-start(bf16[256,128]{1,0:T(8,128)(2,1)S(1)} %convolution_convert_fusion), channel_id=1, source_target_pairs={{0,4},{1,5},{2,6},{3,7},{4,0},{5,1},{6,2},{7,3},{8,12},{9,13},{10,... | collective-permute-start | bytes 196616 | tf_op jit(solution)/shard_map/ppermute | solution.py:224
  4.9 8.3 %collective-permute-start.1 = (bf16[256,128]{1,0:T(8,128)(2,1)S(1)}, bf16[256,128]{1,0:T(8,128)(2,1)S(1)}, u32[]{:S(2)}, u32[]{:S(2)}) collective-permute-start(bf16[256,128]{1,0:T(8,128)(2,1)S(1)} %convolution_convert_fusion), channel_id=1, source_target_pairs={{0,8},{1,9},{2,10},{3,11},{4,12},{5,13},{6,14},{7,15},{8,0},{9,1},... | collective-permute-start | bytes 196616 | tf_op jit(solution)/shard_map/ppermute | solution.py:224
  7.5 6.1 %collective-permute-start.2 = (bf16[256,128]{1,0:T(8,128)(2,1)S(1)}, bf16[256,128]{1,0:T(8,128)(2,1)S(1)}, u32[]{:S(2)}, u32[]{:S(2)}) collective-permute-start(bf16[256,128]{1,0:T(8,128)(2,1)S(1)} %convolution_convert_fusion), channel_id=1, source_target_pairs={{0,12},{1,13},{2,14},{3,15},{4,8},{5,9},{6,10},{7,11},{8,4},{9,5},... | collective-permute-start | bytes 196616 | tf_op jit(solution)/shard_map/ppermute | solution.py:224
  7.5 0.9 %copy-start.2 = (s32[32768]{0:T(1024)S(1)}, s32[32768]{0:T(1024)}, u32[]{:S(2)}) copy-start(s32[32768]{0:T(1024)} %param.8) | copy-start | bytes 393220
  8.4 0.9 %copy-start.3 = (f32[32768]{0:T(1024)S(1)}, f32[32768]{0:T(1024)}, u32[]{:S(2)}) copy-start(f32[32768]{0:T(1024)} %param.9) | copy-start | bytes 393220
  9.3 0.7 %copy-start.4 = (f32[129]{0:T(256)S(1)}, f32[129]{0:T(256)}, u32[]{:S(2)}) copy-start(f32[129]{0:T(256)} %param.10) | copy-start | bytes 1552
  13.6 7.2 %collective-permute-start.3 = (bf16[256,512]{1,0:T(8,128)(2,1)S(1)}, bf16[256,512]{1,0:T(8,128)(2,1)S(1)}, u32[]{:S(2)}, u32[]{:S(2)}) collective-permute-start(bf16[256,512]{1,0:T(8,128)(2,1)S(1)} %pad_maximum_fusion.refs_0_), channel_id=1, source_target_pairs={{0,2},{1,3},{2,0},{3,1},{4,6},{5,7},{6,4},{7,5},{8,10},{9,11},{10,... | collective-permute-start | bytes 786440 | tf_op jit(solution)/shard_map/ppermute | solution.py:224
  15.2 5.7 %collective-permute-start.5 = (bf16[256,512]{1,0:T(8,128)(2,1)S(1)}, bf16[256,512]{1,0:T(8,128)(2,1)S(1)}, u32[]{:S(2)}, u32[]{:S(2)}) collective-permute-start(bf16[256,512]{1,0:T(8,128)(2,1)S(1)} %pad_maximum_fusion.refs_0_), channel_id=1, source_target_pairs={{0,1},{1,0},{2,3},{3,2},{4,5},{5,4},{6,7},{7,6},{8,9},{9,8},{10,11... | collective-permute-start | bytes 786440 | tf_op jit(solution)/shard_map/ppermute | solution.py:224
  18.5 3.9 %copy-start.1 = (f32[9]{0:T(128)S(1)}, f32[9]{0:T(128)}, u32[]{:S(2)}) copy-start(f32[9]{0:T(128)} %slit_ref.1) | copy-start | bytes 112
  20.8 1.5 %collective-permute-start.4 = (bf16[256,512]{1,0:T(8,128)(2,1)S(1)}, bf16[256,512]{1,0:T(8,128)(2,1)S(1)}, u32[]{:S(2)}, u32[]{:S(2)}) collective-permute-start(bf16[256,512]{1,0:T(8,128)(2,1)S(1)} %collective-permute-done.3.refs_2_), channel_id=1, source_target_pairs={{0,1},{1,0},{2,3},{3,2},{4,5},{5,4},{6,7},{7,6},{8,9},{9,8},{10,11... | collective-permute-start | bytes 786440 | tf_op jit(solution)/shard_map/ppermute | solution.py:224

commit v3 on v2

--- a/solution.py
+++ b/solution.py
@@ -239,30 +239,31 @@
         pop = lax.all_gather(pop, "blk", axis=1, tiled=True, axis_index_groups=sets)
 
     lines = (line_level.reshape(-1, 128), line_strength.reshape(-1, 128), inst_wave.reshape(1, -1))
+    early = chunks // 4
     far = [swap(pop, k, count) for k in (4, 8, 12)]
     total = emission_call(
-        functools.partial(first_kernel, chunks=range(chunks // 2), own_levels=own_levels),
+        functools.partial(first_kernel, chunks=range(early), own_levels=own_levels),
         jax.ShapeDtypeStruct((outputs + 2 * REACH, L), F32),
         lines,
-        chunks // 2,
+        early,
     )
     far, total = hold((far, total))
     line = jnp.concatenate([pop] + list(far), axis=1)
     across = swap(line, 2, count)
     line_pair = swap(line, 1, count)
     terms = emission_call(
-        functools.partial(last_kernel, chunks=range(chunks // 2, chunks), own_levels=own_levels),
+        functools.partial(last_kernel, chunks=range(early, chunks), own_levels=own_levels),
         jax.ShapeDtypeStruct((2 * outputs + 4 * REACH, L), BF16),
         lines + (total,),
-        chunks - chunks // 2,
+        chunks - early,
         [pltpu.VMEM((outputs + 2 * REACH, L), F32)],
     )
     across, terms = hold((across, terms))
     across_pair = swap(across, 1, count)
     offsets = [[k ^ offset for k in (0, 4, 8, 12)] for offset in (0, 1, 2, 3)]
-    early = early_products(terms, [line, line_pair, across], offsets[:3])
-    across_pair, early = hold((across_pair, early))
-    image = slit_image(inst_slit, terms, early, [across_pair], offsets[3:])
+    near = early_products(terms, [line, line_pair, across], offsets[:3])
+    across_pair, near = hold((across_pair, near))
+    image = slit_image(inst_slit, terms, near, [across_pair], offsets[3:])
     return join(lax.all_to_all(image, "blk", split_axis=0, concat_axis=0, tiled=True))
 
 

time: 39.4 us -> 37.8 us (0.959)
  waiting for transfers between devices: 3.62 us -> 2.55 us
  blocking collectives: 14.7 us -> 13.7 us
  starting transfers between devices: 7.27 us -> 7.83 us
    ppermute x6, waiting for transfers between devices: 3.62 us -> 2.55 us  [swap(): return lax.ppermute(values, 'blk', [(i, i ^ offset) for i in range(count)])]
    all_to_all x1, blocking collectives: 14.7 us -> 13.7 us  [body(): lax.all_to_all(image, 'blk', split_axis=0, concat_axis=0, tiled=True)]
    ppermute x6, starting transfers between devices: 7.27 us -> 7.83 us  [swap(): return lax.ppermute(values, 'blk', [(i, i ^ offset) for i in range(count)])]
  transfers between devices with their start and end apart: 6 -> 6, of which waited for: 3 -> 3; matrix products, arithmetic and copies ran while one was open for 0% -> 0% of each run, Pallas kernels for 18% -> 19%
where the time goes in v3:
time: 37.8 us; the launch traced here: 37.6 us
  blocking collectives  13.7 us (36%)
  Pallas kernels  8.24 us (22%)
  starting transfers between devices  7.83 us (21%)
  local copies, waits for them, and re-layouts  3.5 us (9%)
  waiting for transfers between devices  2.55 us (7%)
  matrix products  0.91 us (2%)
  other arithmetic  0.8 us (2%)
    all_to_all x1, blocking collectives, body(): lax.all_to_all(image, 'blk', split_axis=0, concat_axis=0, tiled=True)  13.7 us
    ppermute x6, starting transfers between devices, swap(): return lax.ppermute(values, 'blk', [(i, i ^ offset) for i in range(count)])  7.83 us
    pallas_call x2, Pallas kernels, emission_call(): pl.pallas_call(kernel, out_shape=out_shape, in_specs=[VMEM] * len(operand...  6.49 us
    unnamed x10, local copies, waits for them, and re-layouts  3.4 us
    ppermute x6, waiting for transfers between devices, swap(): return lax.ppermute(values, 'blk', [(i, i ^ offset) for i in range(count)])  2.55 us
    pallas_call x1, Pallas kernels, slit_image(): pl.pallas_call(functools.partial(image_kernel, offsets=offsets), out_shap...  1.19 us
    dot_general x1, matrix products, body(): lax.dot_general(onehot, pop_cells, CONTRACT_LAST, preferred_element_type=...  0.91 us
    reshape x1, other arithmetic, join(): return jnp.transpose(image, (1, 0, 2)).reshape(CELL_DEV, count * outputs)  0.77 us
  transfers between devices with their start and end apart: 6, of which 3 were waited for; matrix products, arithmetic and copies ran while one was open for 0% of the time, Pallas kernels for 19%

profile of v3, /device:TPU:0, one launch (start us, length us, event | category | flops | bytes accessed | tf_op | source)
XLA Modules:
  0.0 37.6 jit_solution(16646878474856222925)
XLA Ops:
  0.0 0.9 %copy-done = bf16[128,512]{1,0:T(8,128)(2,1)S(1)} copy-done((bf16[128,512]{1,0:T(8,128)(2,1)S(1)}, bf16[128,512]{1,0:T(8,128)(2,1)}, u32[]{:S(2)}) %copy-start) | copy-done | bytes 131096
  0.9 0.9 %convolution_convert_fusion = bf16[256,128]{1,0:T(8,128)(2,1)S(1)} fusion(bf16[128,512]{1,0:T(8,128)(2,1)S(1)} %copy-done, s32[512]{0:T(512)} %param.7), kind=kOutput, calls=%fused_computation | convolution fusion | flops 33718272 | bytes 198656 | tf_op jit(solution)/shard_map/dot_general | solution.py:236
  1.8 3.1 %collective-permute-start = (bf16[256,128]{1,0:T(8,128)(2,1)S(1)}, bf16[256,128]{1,0:T(8,128)(2,1)S(1)}, u32[]{:S(2)}, u32[]{:S(2)}) collective-permute-start(bf16[256,128]{1,0:T(8,128)(2,1)S(1)} %convolution_convert_fusion), channel_id=1, source_target_pairs={{0,4},{1,5},{2,6},{3,7},{4,0},{5,1},{6,2},{7,3},{8,12},{9,13},{10,... | collective-permute-start | bytes 196616 | tf_op jit(solution)/shard_map/ppermute | solution.py:224
  4.9 2.6 %collective-permute-start.1 = (bf16[256,128]{1,0:T(8,128)(2,1)S(1)}, bf16[256,128]{1,0:T(8,128)(2,1)S(1)}, u32[]{:S(2)}, u32[]{:S(2)}) collective-permute-start(bf16[256,128]{1,0:T(8,128)(2,1)S(1)} %convolution_convert_fusion), channel_id=1, source_target_pairs={{0,8},{1,9},{2,10},{3,11},{4,12},{5,13},{6,14},{7,15},{8,0},{9,1},... | collective-permute-start | bytes 196616 | tf_op jit(solution)/shard_map/ppermute | solution.py:224
  7.5 0.0 collective-permute-start.2
  7.5 0.9 %copy-done.2 = s32[32768]{0:T(1024)S(1)} copy-done((s32[32768]{0:T(1024)S(1)}, s32[32768]{0:T(1024)}, u32[]{:S(2)}) %copy-start.2) | copy-done | bytes 131096
  8.4 0.9 %copy-done.3 = f32[32768]{0:T(1024)S(1)} copy-done((f32[32768]{0:T(1024)S(1)}, f32[32768]{0:T(1024)}, u32[]{:S(2)}) %copy-start.3) | copy-done | bytes 131096
  9.3 0.7 %copy-done.4 = f32[129]{0:T(256)S(1)} copy-done((f32[129]{0:T(256)S(1)}, f32[129]{0:T(256)}, u32[]{:S(2)}) %copy-start.4) | copy-done | bytes 540
  10.0 1.6 %emission.2.given_ref = f32[144,2048]{1,0:T(8,128)S(1)} custom-call(s32[256,128]{1,0:T(8,128)S(1)} %bitcast.10, f32[256,128]{1,0:T(8,128)S(1)} %bitcast.12, f32[1,129]{1,0:T(1,128)S(1)} %bitcast.14), custom_call_target="tpu_custom_call" | custom-call | flops 1073741824 | bytes 65536 | tf_op jit(solution)/shard_map/emission/pallas_call | solution.py:134
  11.6 0.0 collective-permute-done
  11.7 0.5 %collective-permute-done.1 = bf16[256,128]{1,0:T(8,128)(2,1)S(1)} collective-permute-done((bf16[256,128]{1,0:T(8,128)(2,1)S(1)}, bf16[256,128]{1,0:T(8,128)(2,1)S(1)}, u32[]{:S(2)}, u32[]{:S(2)}) %collective-permute-start.1) | collective-permute-done | bytes 65568 | tf_op jit(solution)/shard_map/ppermute | solution.py:224
  12.2 1.4 %collective-permute-done.2 = bf16[256,128]{1,0:T(8,128)(2,1)S(1)} collective-permute-done((bf16[256,128]{1,0:T(8,128)(2,1)S(1)}, bf16[256,128]{1,0:T(8,128)(2,1)S(1)}, u32[]{:S(2)}, u32[]{:S(2)}) %collective-permute-start.2) | collective-permute-done | bytes 65568 | tf_op jit(solution)/shard_map/ppermute | solution.py:224
  13.6 1.6 %collective-permute-start.3 = (bf16[256,512]{1,0:T(8,128)(2,1)S(1)}, bf16[256,512]{1,0:T(8,128)(2,1)S(1)}, u32[]{:S(2)}, u32[]{:S(2)}) collective-permute-start(bf16[256,512]{1,0:T(8,128)(2,1)S(1)} %pad_maximum_fusion.refs_0_), channel_id=1, source_target_pairs={{0,2},{1,3},{2,0},{3,1},{4,6},{5,7},{6,4},{7,5},{8,10},{9,11},{10,... | collective-permute-start | bytes 786440 | tf_op jit(solution)/shard_map/ppermute | solution.py:224
  15.2 0.0 collective-permute-start.5
  15.2 4.8 %emission.3.terms_ref = bf16[288,2048]{1,0:T(8,128)(2,1)S(1)} custom-call(s32[256,128]{1,0:T(8,128)S(1)} %bitcast.11, f32[256,128]{1,0:T(8,128)S(1)} %bitcast.13, f32[1,129]{1,0:T(1,128)S(1)} %bitcast.15, f32[144,2048]{1,0:T(8,128)S(1)} %emission.2.given_ref), custom_call_target="tpu_custom_call" | custom-call | flops 3221225472 | bytes 196608 | tf_op jit(solution)/shard_map/emission/pallas_call | solution.py:134
  20.0 0.0 copy-start.1
  20.1 0.0 collective-permute-done.3.refs_2_
  20.1 0.6 %collective-permute-start.4 = (bf16[256,512]{1,0:T(8,128)(2,1)S(1)}, bf16[256,512]{1,0:T(8,128)(2,1)S(1)}, u32[]{:S(2)}, u32[]{:S(2)}) collective-permute-start(bf16[256,512]{1,0:T(8,128)(2,1)S(1)} %collective-permute-done.3.refs_2_), channel_id=1, source_target_pairs={{0,1},{1,0},{2,3},{3,2},{4,5},{5,4},{6,7},{7,6},{8,9},{9,8},{10,11... | collective-permute-start | bytes 786440 | tf_op jit(solution)/shard_map/ppermute | solution.py:224
  20.7 0.6 %early.1.given_ref = f32[256,288]{1,0:T(8,128)S(1)} custom-call(bf16[288,2048]{1,0:T(8,128)(2,1)S(1)} %emission.3.terms_ref, bf16[256,512]{1,0:T(8,128)(2,1)S(1)} %pad_maximum_fusion.refs_0_, bf16[256,512]{1,0:T(8,128)(2,1)S(1)} %collective-permute-done.5.refs_1_, bf16[256,512]{1,0:T(8,128)(2,1)S(1)} %collective-permute-done.3.refs_2_), custom_call_target="tpu_custom_call" | custom-call | flops 805306368 | bytes 1048576 | tf_op jit(solution)/shard_map/early/pallas_call | solution.py:200
  21.2 0.6 %collective-permute-done.4.refs_0_ = bf16[256,512]{1,0:T(8,128)(2,1)S(1)} collective-permute-done((bf16[256,512]{1,0:T(8,128)(2,1)S(1)}, bf16[256,512]{1,0:T(8,128)(2,1)S(1)}, u32[]{:S(2)}, u32[]{:S(2)}) %collective-permute-start.4) | collective-permute-done | bytes 262176 | tf_op jit(solution)/shard_map/ppermute | solution.py:224
  21.8 1.2 %image.1 = f32[16,24,128]{2,1,0:T(8,128)S(1)} custom-call(f32[9]{0:T(128)S(1)} %copy-done.1, bf16[288,2048]{1,0:T(8,128)(2,1)S(1)} %emission.3.terms_ref, f32[256,288]{1,0:T(8,128)S(1)} %early.1.given_ref, bf16[256,512]{1,0:T(8,128)(2,1)S(1)} %collective-permute-done.4.refs_0_), custom_call_target="tpu_custom_call" | custom-call | flops 268435456 | bytes 1048576 | tf_op jit(solution)/shard_map/image/pallas_call | solution.py:212
  23.0 13.7 %all_to_all.5 = f32[16,24,128]{2,1,0:T(8,128)S(1)} all-to-all(f32[16,24,128]{2,1,0:T(8,128)S(1)} %image.1), channel_id=1, replica_groups=mesh['groups'=2,'blk'=16] {'blk'}, dimensions={0} | all-to-all | bytes 393216 | tf_op jit(solution)/shard_map/all_to_all | solution.py:267
  36.7 0.1 fusion.4
  36.8 0.8 %copy_bitcast_fusion = f32[16,2048]{1,0:T(8,128)} fusion(f32[15,8,8]{2,1,0:T(8,128)S(1)} %get-tuple-element.22, f32[15,8,8]{2,1,0:T(8,128)S(1)} %get-tuple-element.23, f32[15,8,8]{2,1,0:T(8,128)S(1)} %get-tuple-element.24, f32[15,8,8]{2,1,0:T(8,128)S(1)} %get-tuple-element.21, f32[16,24,128]{2,1,0:T(8,128)S(1)} %all_to_all.5), kind=kLoop, calls=%fused_computation.4 | loop fusion | flops 589824 | bytes 507904 | tf_op jit(solution)/shard_map/reshape | solution.py:196
  (7 shorter events, 0.0 us)
Async XLA Ops:
  0.0 0.9 %copy-start = (bf16[128,512]{1,0:T(8,128)(2,1)S(1)}, bf16[128,512]{1,0:T(8,128)(2,1)}, u32[]{:S(2)}) copy-start(bf16[128,512]{1,0:T(8,128)(2,1)} %param.6) | copy-start | bytes 393220
  1.8 9.8 %collective-permute-start = (bf16[256,128]{1,0:T(8,128)(2,1)S(1)}, bf16[256,128]{1,0:T(8,128)(2,1)S(1)}, u32[]{:S(2)}, u32[]{:S(2)}) collective-permute-start(bf16[256,128]{1,0:T(8,128)(2,1)S(1)} %convolution_convert_fusion), channel_id=1, source_target_pairs={{0,4},{1,5},{2,6},{3,7},{4,0},{5,1},{6,2},{7,3},{8,12},{9,13},{10,... | collective-permute-start | bytes 196616 | tf_op jit(solution)/shard_map/ppermute | solution.py:224
  4.9 7.3 %collective-permute-start.1 = (bf16[256,128]{1,0:T(8,128)(2,1)S(1)}, bf16[256,128]{1,0:T(8,128)(2,1)S(1)}, u32[]{:S(2)}, u32[]{:S(2)}) collective-permute-start(bf16[256,128]{1,0:T(8,128)(2,1)S(1)} %convolution_convert_fusion), channel_id=1, source_target_pairs={{0,8},{1,9},{2,10},{3,11},{4,12},{5,13},{6,14},{7,15},{8,0},{9,1},... | collective-permute-start | bytes 196616 | tf_op jit(solution)/shard_map/ppermute | solution.py:224
  7.5 6.1 %collective-permute-start.2 = (bf16[256,128]{1,0:T(8,128)(2,1)S(1)}, bf16[256,128]{1,0:T(8,128)(2,1)S(1)}, u32[]{:S(2)}, u32[]{:S(2)}) collective-permute-start(bf16[256,128]{1,0:T(8,128)(2,1)S(1)} %convolution_convert_fusion), channel_id=1, source_target_pairs={{0,12},{1,13},{2,14},{3,15},{4,8},{5,9},{6,10},{7,11},{8,4},{9,5},... | collective-permute-start | bytes 196616 | tf_op jit(solution)/shard_map/ppermute | solution.py:224
  7.5 0.9 %copy-start.2 = (s32[32768]{0:T(1024)S(1)}, s32[32768]{0:T(1024)}, u32[]{:S(2)}) copy-start(s32[32768]{0:T(1024)} %param.8) | copy-start | bytes 393220
  8.4 0.9 %copy-start.3 = (f32[32768]{0:T(1024)S(1)}, f32[32768]{0:T(1024)}, u32[]{:S(2)}) copy-start(f32[32768]{0:T(1024)} %param.9) | copy-start | bytes 393220
  9.3 0.7 %copy-start.4 = (f32[129]{0:T(256)S(1)}, f32[129]{0:T(256)}, u32[]{:S(2)}) copy-start(f32[129]{0:T(256)} %param.10) | copy-start | bytes 1552
  13.6 6.5 %collective-permute-start.3 = (bf16[256,512]{1,0:T(8,128)(2,1)S(1)}, bf16[256,512]{1,0:T(8,128)(2,1)S(1)}, u32[]{:S(2)}, u32[]{:S(2)}) collective-permute-start(bf16[256,512]{1,0:T(8,128)(2,1)S(1)} %pad_maximum_fusion.refs_0_), channel_id=1, source_target_pairs={{0,2},{1,3},{2,0},{3,1},{4,6},{5,7},{6,4},{7,5},{8,10},{9,11},{10,... | collective-permute-start | bytes 786440 | tf_op jit(solution)/shard_map/ppermute | solution.py:224
  15.2 5.5 %collective-permute-start.5 = (bf16[256,512]{1,0:T(8,128)(2,1)S(1)}, bf16[256,512]{1,0:T(8,128)(2,1)S(1)}, u32[]{:S(2)}, u32[]{:S(2)}) collective-permute-start(bf16[256,512]{1,0:T(8,128)(2,1)S(1)} %pad_maximum_fusion.refs_0_), channel_id=1, source_target_pairs={{0,1},{1,0},{2,3},{3,2},{4,5},{5,4},{6,7},{7,6},{8,9},{9,8},{10,11... | collective-permute-start | bytes 786440 | tf_op jit(solution)/shard_map/ppermute | solution.py:224
  20.0 1.8 %copy-start.1 = (f32[9]{0:T(128)S(1)}, f32[9]{0:T(128)}, u32[]{:S(2)}) copy-start(f32[9]{0:T(128)} %slit_ref.1) | copy-start | bytes 112
  20.1 1.7 %collective-permute-start.4 = (bf16[256,512]{1,0:T(8,128)(2,1)S(1)}, bf16[256,512]{1,0:T(8,128)(2,1)S(1)}, u32[]{:S(2)}, u32[]{:S(2)}) collective-permute-start(bf16[256,512]{1,0:T(8,128)(2,1)S(1)} %collective-permute-done.3.refs_2_), channel_id=1, source_target_pairs={{0,1},{1,0},{2,3},{3,2},{4,5},{5,4},{6,7},{7,6},{8,9},{9,8},{10,11... | collective-permute-start | bytes 786440 | tf_op jit(solution)/shard_map/ppermute | solution.py:224

commit v4 on v3

--- a/solution.py
+++ b/solution.py
@@ -19,7 +19,7 @@
 SPAN = CHUNK_OUT + 2 * REACH
 CHUNK_ROWS = CHUNK * LINES_BIN // 128
 TAP_WIDTH = 512
-UNROLL = 4
+UNROLL = 16
 BF16 = jnp.bfloat16
 F32 = jnp.float32
 VMEM_LIMIT = 48 * 1024 * 1024
@@ -152,8 +152,8 @@
 
     for pop_ref, own in zip(pop_refs, offsets):
         for i in range(0, len(own), 2):
-            terms = jnp.concatenate([block(own[i]), block(own[i + 1])], axis=1)
-            pop = pop_ref[:, i * LOW : (i + 2) * LOW]
+            terms = jnp.concatenate([block(offset) for offset in own[i : i + 2]], axis=1)
+            pop = pop_ref[:, i * LOW : i * LOW + terms.shape[1]]
             new = lax.dot_general(pop, terms, CONTRACT_LAST, preferred_element_type=F32)
             total = new if total is None else total + new
     return total
@@ -241,16 +241,18 @@
     lines = (line_level.reshape(-1, 128), line_strength.reshape(-1, 128), inst_wave.reshape(1, -1))
     early = chunks // 4
     far = [swap(pop, k, count) for k in (4, 8, 12)]
+    beside = swap(pop, 2, count)
     total = emission_call(
         functools.partial(first_kernel, chunks=range(early), own_levels=own_levels),
         jax.ShapeDtypeStruct((outputs + 2 * REACH, L), F32),
         lines,
         early,
     )
-    far, total = hold((far, total))
-    line = jnp.concatenate([pop] + list(far), axis=1)
+    far, beside, total = hold((far, beside, total))
+    line = jnp.concatenate(list(far), axis=1)
     across = swap(line, 2, count)
-    line_pair = swap(line, 1, count)
+    near = jnp.concatenate([pop, beside], axis=1)
+    line_pair, near_pair = swap(line, 1, count), swap(near, 1, count)
     terms = emission_call(
         functools.partial(last_kernel, chunks=range(early, chunks), own_levels=own_levels),
         jax.ShapeDtypeStruct((2 * outputs + 4 * REACH, L), BF16),
@@ -260,10 +262,14 @@
     )
     across, terms = hold((across, terms))
     across_pair = swap(across, 1, count)
-    offsets = [[k ^ offset for k in (0, 4, 8, 12)] for offset in (0, 1, 2, 3)]
-    near = early_products(terms, [line, line_pair, across], offsets[:3])
-    across_pair, near = hold((across_pair, near))
-    image = slit_image(inst_slit, terms, near, [across_pair], offsets[3:])
+    z = [4, 8, 12]
+    first = early_products(
+        terms,
+        [near, line, line_pair, near_pair, across],
+        [[0, 2], z, [k ^ 1 for k in z], [1, 3], [k ^ 2 for k in z]],
+    )
+    across_pair, first = hold((across_pair, first))
+    image = slit_image(inst_slit, terms, first, [across_pair], [[k ^ 3 for k in z]])
     return join(lax.all_to_all(image, "blk", split_axis=0, concat_axis=0, tiled=True))
 
 

time: 37.8 us -> 36.2 us (0.958)
  Pallas kernels: 8.24 us -> 5.5 us
  starting transfers between devices: 7.83 us -> 9.58 us
  blocking collectives: 13.7 us -> 13.1 us
    pallas_call x2, Pallas kernels: 6.49 us -> 3.65 us  [emission_call(): pl.pallas_call(kernel, out_shape=out_shape, in_specs=[VMEM] * len(operand...]
    ppermute x6 -> x8, starting transfers between devices: 7.83 us -> 9.58 us  [swap(): return lax.ppermute(values, 'blk', [(i, i ^ offset) for i in range(count)])]
    all_to_all x1, blocking collectives: 13.7 us -> 13.1 us  [body(): lax.all_to_all(image, 'blk', split_axis=0, concat_axis=0, tiled=True)]
    ppermute x6 -> x8, waiting for transfers between devices: 2.55 us -> 2.46 us  [swap(): return lax.ppermute(values, 'blk', [(i, i ^ offset) for i in range(count)])]
    unnamed x10 -> x12, local copies, waits for them, and re-layouts: 3.4 us -> 3.43 us
  transfers between devices with their start and end apart: 6 -> 8, of which waited for: 3 -> 3; matrix products, arithmetic and copies ran while one was open for 0% -> 0% of each run, Pallas kernels for 19% -> 12%
where the time goes in v4:
time: 36.2 us; the launch traced here: 36 us
  blocking collectives  13.1 us (36%)
  starting transfers between devices  9.58 us (26%)
  Pallas kernels  5.5 us (15%)
  local copies, waits for them, and re-layouts  3.55 us (10%)
  waiting for transfers between devices  2.46 us (7%)
  matrix products  0.91 us (3%)
  other arithmetic  0.79 us (2%)
    all_to_all x1, blocking collectives, body(): lax.all_to_all(image, 'blk', split_axis=0, concat_axis=0, tiled=True)  13.1 us
    ppermute x8, starting transfers between devices, swap(): return lax.ppermute(values, 'blk', [(i, i ^ offset) for i in range(count)])  9.58 us
    pallas_call x2, Pallas kernels, emission_call(): pl.pallas_call(kernel, out_shape=out_shape, in_specs=[VMEM] * len(operand...  3.65 us
    unnamed x12, local copies, waits for them, and re-layouts  3.43 us
    ppermute x8, waiting for transfers between devices, swap(): return lax.ppermute(values, 'blk', [(i, i ^ offset) for i in range(count)])  2.46 us
    pallas_call x1, Pallas kernels, slit_image(): pl.pallas_call(functools.partial(image_kernel, offsets=offsets), out_shap...  1.16 us
    dot_general x1, matrix products, body(): lax.dot_general(onehot, pop_cells, CONTRACT_LAST, preferred_element_type=...  0.91 us
    reshape x1, other arithmetic, join(): return jnp.transpose(image, (1, 0, 2)).reshape(CELL_DEV, count * outputs)  0.77 us
  transfers between devices with their start and end apart: 8, of which 3 were waited for; matrix products, arithmetic and copies ran while one was open for 0% of the time, Pallas kernels for 12%

profile of v4, /device:TPU:0, one launch (start us, length us, event | category | flops | bytes accessed | tf_op | source)
XLA Modules:
  0.0 36.0 jit_solution(6066217898011420713)
XLA Ops:
  0.0 0.9 %copy-done = bf16[128,512]{1,0:T(8,128)(2,1)S(1)} copy-done((bf16[128,512]{1,0:T(8,128)(2,1)S(1)}, bf16[128,512]{1,0:T(8,128)(2,1)}, u32[]{:S(2)}) %copy-start) | copy-done | bytes 131096
  0.9 0.9 %convolution_convert_fusion = bf16[256,128]{1,0:T(8,128)(2,1)S(1)} fusion(bf16[128,512]{1,0:T(8,128)(2,1)S(1)} %copy-done, s32[512]{0:T(512)} %param.7), kind=kOutput, calls=%fused_computation | convolution fusion | flops 33718272 | bytes 198656 | tf_op jit(solution)/shard_map/dot_general | solution.py:236
  1.8 3.1 %collective-permute-start = (bf16[256,128]{1,0:T(8,128)(2,1)S(1)}, bf16[256,128]{1,0:T(8,128)(2,1)S(1)}, u32[]{:S(2)}, u32[]{:S(2)}) collective-permute-start(bf16[256,128]{1,0:T(8,128)(2,1)S(1)} %convolution_convert_fusion), channel_id=1, source_target_pairs={{0,4},{1,5},{2,6},{3,7},{4,0},{5,1},{6,2},{7,3},{8,12},{9,13},{10,... | collective-permute-start | bytes 196616 | tf_op jit(solution)/shard_map/ppermute | solution.py:224
  4.9 2.6 %collective-permute-start.1 = (bf16[256,128]{1,0:T(8,128)(2,1)S(1)}, bf16[256,128]{1,0:T(8,128)(2,1)S(1)}, u32[]{:S(2)}, u32[]{:S(2)}) collective-permute-start(bf16[256,128]{1,0:T(8,128)(2,1)S(1)} %convolution_convert_fusion), channel_id=1, source_target_pairs={{0,8},{1,9},{2,10},{3,11},{4,12},{5,13},{6,14},{7,15},{8,0},{9,1},... | collective-permute-start | bytes 196616 | tf_op jit(solution)/shard_map/ppermute | solution.py:224
  7.5 0.0 collective-permute-start.2
  7.5 1.7 %collective-permute-start.3 = (bf16[256,128]{1,0:T(8,128)(2,1)S(1)}, bf16[256,128]{1,0:T(8,128)(2,1)S(1)}, u32[]{:S(2)}, u32[]{:S(2)}) collective-permute-start(bf16[256,128]{1,0:T(8,128)(2,1)S(1)} %convolution_convert_fusion), channel_id=1, source_target_pairs={{0,2},{1,3},{2,0},{3,1},{4,6},{5,7},{6,4},{7,5},{8,10},{9,11},{10,... | collective-permute-start | bytes 196616 | tf_op jit(solution)/shard_map/ppermute | solution.py:224
  9.2 0.9 %copy-done.2 = s32[32768]{0:T(1024)S(1)} copy-done((s32[32768]{0:T(1024)S(1)}, s32[32768]{0:T(1024)}, u32[]{:S(2)}) %copy-start.2) | copy-done | bytes 131096
  10.1 0.9 %copy-done.3 = f32[32768]{0:T(1024)S(1)} copy-done((f32[32768]{0:T(1024)S(1)}, f32[32768]{0:T(1024)}, u32[]{:S(2)}) %copy-start.3) | copy-done | bytes 131096
  11.1 0.7 %copy-done.4 = f32[129]{0:T(256)S(1)} copy-done((f32[129]{0:T(256)S(1)}, f32[129]{0:T(256)}, u32[]{:S(2)}) %copy-start.4) | copy-done | bytes 540
  11.7 1.0 %emission.2.given_ref = f32[144,2048]{1,0:T(8,128)S(1)} custom-call(s32[256,128]{1,0:T(8,128)S(1)} %bitcast.10, f32[256,128]{1,0:T(8,128)S(1)} %bitcast.12, f32[1,129]{1,0:T(1,128)S(1)} %bitcast.14), custom_call_target="tpu_custom_call" | custom-call | flops 1073741824 | bytes 65536 | tf_op jit(solution)/shard_map/emission/pallas_call | solution.py:134
  12.7 0.0 collective-permute-done.1
  12.8 0.8 %collective-permute-done.2 = bf16[256,128]{1,0:T(8,128)(2,1)S(1)} collective-permute-done((bf16[256,128]{1,0:T(8,128)(2,1)S(1)}, bf16[256,128]{1,0:T(8,128)(2,1)S(1)}, u32[]{:S(2)}, u32[]{:S(2)}) %collective-permute-start.2) | collective-permute-done | bytes 65568 | tf_op jit(solution)/shard_map/ppermute | solution.py:224
  13.6 0.0 collective-permute-done.3
  13.6 1.6 %collective-permute-start.4 = (bf16[256,384]{1,0:T(8,128)(2,1)S(1)}, bf16[256,384]{1,0:T(8,128)(2,1)S(1)}, u32[]{:S(2)}, u32[]{:S(2)}) collective-permute-start(bf16[256,384]{1,0:T(8,128)(2,1)S(1)} %constant_dynamic-update-slice_fusion.refs_1_), channel_id=1, source_target_pairs={{0,2},{1,3},{2,0},{3,1},{4,6},{5,7},{6,4},{7,5},{8,10},{9,11},{10,... | collective-permute-start | bytes 589832 | tf_op jit(solution)/shard_map/ppermute | solution.py:224
  15.3 0.6 %collective-permute-start.7 = (bf16[256,256]{1,0:T(8,128)(2,1)S(1)}, bf16[256,256]{1,0:T(8,128)(2,1)S(1)}, u32[]{:S(2)}, u32[]{:S(2)}) collective-permute-start(bf16[256,256]{1,0:T(8,128)(2,1)S(1)} %pad_maximum_fusion.refs_0_), channel_id=1, source_target_pairs={{0,1},{1,0},{2,3},{3,2},{4,5},{5,4},{6,7},{7,6},{8,9},{9,8},{10,11... | collective-permute-start | bytes 393224 | tf_op jit(solution)/shard_map/ppermute | solution.py:224
  15.8 2.6 %emission.3.terms_ref = bf16[288,2048]{1,0:T(8,128)(2,1)S(1)} custom-call(s32[256,128]{1,0:T(8,128)S(1)} %bitcast.11, f32[256,128]{1,0:T(8,128)S(1)} %bitcast.13, f32[1,129]{1,0:T(1,128)S(1)} %bitcast.15, f32[144,2048]{1,0:T(8,128)S(1)} %emission.2.given_ref), custom_call_target="tpu_custom_call" | custom-call | flops 3221225472 | bytes 196608 | tf_op jit(solution)/shard_map/emission/pallas_call | solution.py:134
  18.5 0.0 copy-start.1
  18.5 0.9 %collective-permute-done.4.refs_4_ = bf16[256,384]{1,0:T(8,128)(2,1)S(1)} collective-permute-done((bf16[256,384]{1,0:T(8,128)(2,1)S(1)}, bf16[256,384]{1,0:T(8,128)(2,1)S(1)}, u32[]{:S(2)}, u32[]{:S(2)}) %collective-permute-start.4) | collective-permute-done | bytes 196640 | tf_op jit(solution)/shard_map/ppermute | solution.py:224
  19.4 0.7 %early.1.given_ref = f32[256,288]{1,0:T(8,128)S(1)} custom-call(bf16[288,2048]{1,0:T(8,128)(2,1)S(1)} %emission.3.terms_ref, bf16[256,256]{1,0:T(8,128)(2,1)S(1)} %pad_maximum_fusion.refs_0_, bf16[256,384]{1,0:T(8,128)(2,1)S(1)} %constant_dynamic-update-slice_fusion.refs_1_, bf16[256,384]{1,0:T(8,128)(2,1)S(1)} %collective-permute-done.6.refs_2_, ...), custom_call_target="tpu_custom_call" | custom-call | flops 805306368 | bytes 1048576 | tf_op jit(solution)/shard_map/early/pallas_call | solution.py:200
  20.1 0.7 %collective-permute-done.5.refs_0_ = bf16[256,384]{1,0:T(8,128)(2,1)S(1)} collective-permute-done((bf16[256,384]{1,0:T(8,128)(2,1)S(1)}, bf16[256,384]{1,0:T(8,128)(2,1)S(1)}, u32[]{:S(2)}, u32[]{:S(2)}) %collective-permute-start.5) | collective-permute-done | bytes 196640 | tf_op jit(solution)/shard_map/ppermute | solution.py:224
  20.8 1.2 %image.1 = f32[16,24,128]{2,1,0:T(8,128)S(1)} custom-call(f32[9]{0:T(128)S(1)} %copy-done.1, bf16[288,2048]{1,0:T(8,128)(2,1)S(1)} %emission.3.terms_ref, f32[256,288]{1,0:T(8,128)S(1)} %early.1.given_ref, bf16[256,384]{1,0:T(8,128)(2,1)S(1)} %collective-permute-done.5.refs_0_), custom_call_target="tpu_custom_call" | custom-call | flops 268435456 | bytes 1048576 | tf_op jit(solution)/shard_map/image/pallas_call | solution.py:212
  22.0 13.1 %all_to_all.5 = f32[16,24,128]{2,1,0:T(8,128)S(1)} all-to-all(f32[16,24,128]{2,1,0:T(8,128)S(1)} %image.1), channel_id=1, replica_groups=mesh['groups'=2,'blk'=16] {'blk'}, dimensions={0} | all-to-all | bytes 393216 | tf_op jit(solution)/shard_map/all_to_all | solution.py:273
  35.1 0.1 fusion.4
  35.2 0.8 %copy_bitcast_fusion = f32[16,2048]{1,0:T(8,128)} fusion(f32[15,8,8]{2,1,0:T(8,128)S(1)} %get-tuple-element.24, f32[15,8,8]{2,1,0:T(8,128)S(1)} %get-tuple-element.25, f32[15,8,8]{2,1,0:T(8,128)S(1)} %get-tuple-element.26, f32[15,8,8]{2,1,0:T(8,128)S(1)} %get-tuple-element.23, f32[16,24,128]{2,1,0:T(8,128)S(1)} %all_to_all.5), kind=kLoop, calls=%fused_computation.3 | loop fusion | flops 589824 | bytes 507904 | tf_op jit(solution)/shard_map/reshape | solution.py:196
  (14 shorter events, 0.1 us)
Async XLA Ops:
  0.0 0.9 %copy-start = (bf16[128,512]{1,0:T(8,128)(2,1)S(1)}, bf16[128,512]{1,0:T(8,128)(2,1)}, u32[]{:S(2)}) copy-start(bf16[128,512]{1,0:T(8,128)(2,1)} %param.6) | copy-start | bytes 393220
  1.8 10.9 %collective-permute-start = (bf16[256,128]{1,0:T(8,128)(2,1)S(1)}, bf16[256,128]{1,0:T(8,128)(2,1)S(1)}, u32[]{:S(2)}, u32[]{:S(2)}) collective-permute-start(bf16[256,128]{1,0:T(8,128)(2,1)S(1)} %convolution_convert_fusion), channel_id=1, source_target_pairs={{0,4},{1,5},{2,6},{3,7},{4,0},{5,1},{6,2},{7,3},{8,12},{9,13},{10,... | collective-permute-start | bytes 196616 | tf_op jit(solution)/shard_map/ppermute | solution.py:224
  4.9 7.8 %collective-permute-start.1 = (bf16[256,128]{1,0:T(8,128)(2,1)S(1)}, bf16[256,128]{1,0:T(8,128)(2,1)S(1)}, u32[]{:S(2)}, u32[]{:S(2)}) collective-permute-start(bf16[256,128]{1,0:T(8,128)(2,1)S(1)} %convolution_convert_fusion), channel_id=1, source_target_pairs={{0,8},{1,9},{2,10},{3,11},{4,12},{5,13},{6,14},{7,15},{8,0},{9,1},... | collective-permute-start | bytes 196616 | tf_op jit(solution)/shard_map/ppermute | solution.py:224
  7.5 6.1 %collective-permute-start.2 = (bf16[256,128]{1,0:T(8,128)(2,1)S(1)}, bf16[256,128]{1,0:T(8,128)(2,1)S(1)}, u32[]{:S(2)}, u32[]{:S(2)}) collective-permute-start(bf16[256,128]{1,0:T(8,128)(2,1)S(1)} %convolution_convert_fusion), channel_id=1, source_target_pairs={{0,12},{1,13},{2,14},{3,15},{4,8},{5,9},{6,10},{7,11},{8,4},{9,5},... | collective-permute-start | bytes 196616 | tf_op jit(solution)/shard_map/ppermute | solution.py:224
  7.5 6.1 %collective-permute-start.3 = (bf16[256,128]{1,0:T(8,128)(2,1)S(1)}, bf16[256,128]{1,0:T(8,128)(2,1)S(1)}, u32[]{:S(2)}, u32[]{:S(2)}) collective-permute-start(bf16[256,128]{1,0:T(8,128)(2,1)S(1)} %convolution_convert_fusion), channel_id=1, source_target_pairs={{0,2},{1,3},{2,0},{3,1},{4,6},{5,7},{6,4},{7,5},{8,10},{9,11},{10,... | collective-permute-start | bytes 196616 | tf_op jit(solution)/shard_map/ppermute | solution.py:224
  9.2 0.9 %copy-start.2 = (s32[32768]{0:T(1024)S(1)}, s32[32768]{0:T(1024)}, u32[]{:S(2)}) copy-start(s32[32768]{0:T(1024)} %param.8) | copy-start | bytes 393220
  10.1 0.9 %copy-start.3 = (f32[32768]{0:T(1024)S(1)}, f32[32768]{0:T(1024)}, u32[]{:S(2)}) copy-start(f32[32768]{0:T(1024)} %param.9) | copy-start | bytes 393220
  11.1 0.7 %copy-start.4 = (f32[129]{0:T(256)S(1)}, f32[129]{0:T(256)}, u32[]{:S(2)}) copy-start(f32[129]{0:T(256)} %param.10) | copy-start | bytes 1552
  13.6 5.7 %collective-permute-start.4 = (bf16[256,384]{1,0:T(8,128)(2,1)S(1)}, bf16[256,384]{1,0:T(8,128)(2,1)S(1)}, u32[]{:S(2)}, u32[]{:S(2)}) collective-permute-start(bf16[256,384]{1,0:T(8,128)(2,1)S(1)} %constant_dynamic-update-slice_fusion.refs_1_), channel_id=1, source_target_pairs={{0,2},{1,3},{2,0},{3,1},{4,6},{5,7},{6,4},{7,5},{8,10},{9,11},{10,... | collective-permute-start | bytes 589832 | tf_op jit(solution)/shard_map/ppermute | solution.py:224
  15.2 4.2 %collective-permute-start.6 = (bf16[256,384]{1,0:T(8,128)(2,1)S(1)}, bf16[256,384]{1,0:T(8,128)(2,1)S(1)}, u32[]{:S(2)}, u32[]{:S(2)}) collective-permute-start(bf16[256,384]{1,0:T(8,128)(2,1)S(1)} %constant_dynamic-update-slice_fusion.refs_1_), channel_id=1, source_target_pairs={{0,1},{1,0},{2,3},{3,2},{4,5},{5,4},{6,7},{7,6},{8,9},{9,8},{10,11... | collective-permute-start | bytes 589832 | tf_op jit(solution)/shard_map/ppermute | solution.py:224
  15.3 4.1 %collective-permute-start.7 = (bf16[256,256]{1,0:T(8,128)(2,1)S(1)}, bf16[256,256]{1,0:T(8,128)(2,1)S(1)}, u32[]{:S(2)}, u32[]{:S(2)}) collective-permute-start(bf16[256,256]{1,0:T(8,128)(2,1)S(1)} %pad_maximum_fusion.refs_0_), channel_id=1, source_target_pairs={{0,1},{1,0},{2,3},{3,2},{4,5},{5,4},{6,7},{7,6},{8,9},{9,8},{10,11... | collective-permute-start | bytes 393224 | tf_op jit(solution)/shard_map/ppermute | solution.py:224
  18.5 2.3 %copy-start.1 = (f32[9]{0:T(128)S(1)}, f32[9]{0:T(128)}, u32[]{:S(2)}) copy-start(f32[9]{0:T(128)} %slit_ref.1) | copy-start | bytes 112
  19.4 1.4 %collective-permute-start.5 = (bf16[256,384]{1,0:T(8,128)(2,1)S(1)}, bf16[256,384]{1,0:T(8,128)(2,1)S(1)}, u32[]{:S(2)}, u32[]{:S(2)}) collective-permute-start(bf16[256,384]{1,0:T(8,128)(2,1)S(1)} %collective-permute-done.4.refs_4_), channel_id=1, source_target_pairs={{0,1},{1,0},{2,3},{3,2},{4,5},{5,4},{6,7},{7,6},{8,9},{9,8},{10,11... | collective-permute-start | bytes 589832 | tf_op jit(solution)/shard_map/ppermute | solution.py:224

commit v5 on v4

--- a/solution.py
+++ b/solution.py
@@ -19,13 +19,14 @@
 SPAN = CHUNK_OUT + 2 * REACH
 CHUNK_ROWS = CHUNK * LINES_BIN // 128
 TAP_WIDTH = 512
+TAP_FLOPS = 1 << 32
 UNROLL = 16
+EARLY = 1
 BF16 = jnp.bfloat16
 F32 = jnp.float32
 VMEM_LIMIT = 48 * 1024 * 1024
 CONTRACT_LAST = (((1,), (1,)), ((), ()))
 VMEM = pl.BlockSpec(memory_space=pltpu.VMEM)
-SMEM = pl.BlockSpec(memory_space=pltpu.SMEM)
 
 
 def two_terms(values):
@@ -33,12 +34,25 @@
     return first, (values - first.astype(F32)).astype(BF16)
 
 
-def tap_matrix(wave_ref, tap_ref):
+def tap_kernel(wave_ref, out_ref, tap_ref):
     tap_ref[...] = jnp.zeros_like(tap_ref)
     tap_ref[:, : wave_ref.shape[1]] = jnp.broadcast_to(wave_ref[...], (8, wave_ref.shape[1]))
     base = jnp.concatenate([tap_ref[...]] * (SPAN // 8), axis=0)
     taps = pltpu.roll(base, TAP_WIDTH - 128, 1, stride=BINS, stride_axis=0)[:, :CHUNK]
-    return taps
+    first, second = two_terms(taps)
+    out_ref[:SPAN, :] = first
+    out_ref[SPAN:, :] = second
+
+
+def tap_matrix(wave):
+    return pl.pallas_call(
+        tap_kernel,
+        out_shape=jax.ShapeDtypeStruct((2 * SPAN, CHUNK), BF16),
+        in_specs=[VMEM],
+        scratch_shapes=[pltpu.VMEM((8, TAP_WIDTH), F32)],
+        cost_estimate=pl.CostEstimate(flops=TAP_FLOPS, bytes_accessed=1 << 16, transcendentals=0),
+        name="taps",
+    )(wave)
 
 
 def emission(lines, own_levels, scratch):
@@ -90,9 +104,8 @@
 
 
 def blurred(taps, em):
-    rows = taps.shape[0]
-    both = jnp.dot(jnp.concatenate(two_terms(taps), axis=0), em, preferred_element_type=F32)
-    return both[:rows] + both[rows:]
+    both = jnp.dot(taps, em, preferred_element_type=F32)
+    return both[:SPAN] + both[SPAN:]
 
 
 def add_chunks(total_ref, chunks, taps, level_ref, strength_ref, own_levels, scratch):
@@ -102,19 +115,17 @@
         total_ref[place, :] += blurred(taps, scratch[-1][...])
 
 
-def first_kernel(level_ref, strength_ref, wave_ref, total_ref, tap_ref, *scratch, chunks, own_levels):
+def first_kernel(level_ref, strength_ref, taps_ref, total_ref, *scratch, chunks, own_levels):
     total_ref[...] = jnp.zeros_like(total_ref)
-    taps = tap_matrix(wave_ref, tap_ref)
-    add_chunks(total_ref, chunks, taps, level_ref, strength_ref, own_levels, scratch)
+    add_chunks(total_ref, chunks, taps_ref[...], level_ref, strength_ref, own_levels, scratch)
 
 
 def last_kernel(
-    level_ref, strength_ref, wave_ref, given_ref, out_ref, total_ref, tap_ref, *scratch, chunks, own_levels
+    level_ref, strength_ref, taps_ref, given_ref, out_ref, total_ref, *scratch, chunks, own_levels
 ):
     outputs = total_ref.shape[0] - 2 * REACH
     total_ref[...] = given_ref[...]
-    taps = tap_matrix(wave_ref, tap_ref)
-    add_chunks(total_ref, chunks, taps, level_ref, strength_ref, own_levels, scratch)
+    add_chunks(total_ref, chunks, taps_ref[...], level_ref, strength_ref, own_levels, scratch)
     first, second = two_terms(total_ref[REACH : REACH + outputs, :])
     out_ref[:outputs, :] = first
     out_ref[outputs : 2 * outputs, :] = second
@@ -126,7 +137,6 @@
 
 def emission_call(kernel, out_shape, operands, chunks, extra=()):
     scratch = [
-        pltpu.VMEM((8, TAP_WIDTH), F32),
         pltpu.VMEM((CHUNK_ROWS, 128), F32),
         pltpu.VMEM((CHUNK_ROWS, 128), F32),
         pltpu.VMEM((CHUNK, L), BF16),
@@ -138,7 +148,7 @@
         scratch_shapes=list(extra) + scratch,
         compiler_params=pltpu.CompilerParams(vmem_limit_bytes=VMEM_LIMIT),
         cost_estimate=pl.CostEstimate(
-            flops=2 * chunks * CHUNK * L * 1024, bytes_accessed=chunks * CHUNK * 256, transcendentals=0
+            flops=2 * chunks * CHUNK * L * 32, bytes_accessed=chunks * CHUNK * 256, transcendentals=0
         ),
         name="emission",
     )(*operands)
@@ -174,9 +184,9 @@
     pad_ref[8 : 8 + cells, outputs : outputs + edge] = (
         total[:, 2 * outputs : 2 * outputs + edge] + total[:, 2 * outputs + edge :]
     )
-    image = slit_ref[0] * pad_ref[4 : 4 + cells, :]
+    image = slit_ref[:, 0:1] * pad_ref[4 : 4 + cells, :]
     for tap in range(1, 9):
-        image += slit_ref[tap] * pad_ref[4 + tap : 4 + tap + cells, :]
+        image += slit_ref[:, tap : tap + 1] * pad_ref[4 + tap : 4 + tap + cells, :]
     lane = lax.broadcasted_iota(jnp.int32, (8, 128), 1)
     for place in range(cells // CELL_DEV):
         own = image[place * CELL_DEV : (place + 1) * CELL_DEV]
@@ -212,7 +222,7 @@
     return pl.pallas_call(
         functools.partial(image_kernel, offsets=offsets),
         out_shape=jax.ShapeDtypeStruct((cells // CELL_DEV, CELL_DEV + 8, outputs), F32),
-        in_specs=[SMEM] + [VMEM] * (2 + len(pops)),
+        in_specs=[VMEM] * (3 + len(pops)),
         scratch_shapes=[pltpu.VMEM((cells + 16, outputs + 128), F32)],
         compiler_params=pltpu.CompilerParams(vmem_limit_bytes=VMEM_LIMIT),
         cost_estimate=pl.CostEstimate(flops=1 << 28, bytes_accessed=1 << 20, transcendentals=0),
@@ -238,8 +248,8 @@
         sets = [list(range(i, count, HIGH)) for i in range(HIGH)]
         pop = lax.all_gather(pop, "blk", axis=1, tiled=True, axis_index_groups=sets)
 
-    lines = (line_level.reshape(-1, 128), line_strength.reshape(-1, 128), inst_wave.reshape(1, -1))
-    early = chunks // 4
+    lines = (line_level.reshape(-1, 128), line_strength.reshape(-1, 128), tap_matrix(inst_wave.reshape(1, -1)))
+    early = EARLY
     far = [swap(pop, k, count) for k in (4, 8, 12)]
     beside = swap(pop, 2, count)
     total = emission_call(
@@ -249,10 +259,11 @@
         early,
     )
     far, beside, total = hold((far, beside, total))
-    line = jnp.concatenate(list(far), axis=1)
-    across = swap(line, 2, count)
-    near = jnp.concatenate([pop, beside], axis=1)
-    line_pair, near_pair = swap(line, 1, count), swap(near, 1, count)
+    pair, beside = hold((jnp.concatenate(far[1:], axis=1), beside))
+    across = swap(pair, 2, count)
+    corner = swap(beside, 4, count)
+    near = jnp.concatenate([pop, beside] + list(far), axis=1)
+    near_pair = swap(near, 1, count)
     terms = emission_call(
         functools.partial(last_kernel, chunks=range(early, chunks), own_levels=own_levels),
         jax.ShapeDtypeStruct((2 * outputs + 4 * REACH, L), BF16),
@@ -260,16 +271,12 @@
         chunks - early,
         [pltpu.VMEM((outputs + 2 * REACH, L), F32)],
     )
-    across, terms = hold((across, terms))
-    across_pair = swap(across, 1, count)
-    z = [4, 8, 12]
-    first = early_products(
-        terms,
-        [near, line, line_pair, near_pair, across],
-        [[0, 2], z, [k ^ 1 for k in z], [1, 3], [k ^ 2 for k in z]],
-    )
-    across_pair, first = hold((across_pair, first))
-    image = slit_image(inst_slit, terms, first, [across_pair], [[k ^ 3 for k in z]])
+    across, corner, terms = hold((across, corner, terms))
+    rest = jnp.concatenate([across, corner], axis=1)
+    rest_pair = swap(rest, 1, count)
+    first = early_products(terms, [near, near_pair, rest], [[0, 2, 4, 8, 12], [1, 3, 5, 9, 13], [10, 14, 6]])
+    rest_pair, first = hold((rest_pair, first))
+    image = slit_image(inst_slit.reshape(1, -1), terms, first, [rest_pair], [[11, 15, 7]])
     return join(lax.all_to_all(image, "blk", split_axis=0, concat_axis=0, tiled=True))
 
 

time: 36.2 us -> 35.6 us (0.983)
  local copies, waits for them, and re-layouts: 3.55 us -> 1.93 us
  Pallas kernels: 5.5 us -> 6.49 us
  waiting for transfers between devices: 2.46 us -> 3.25 us
  starting transfers between devices: 9.58 us -> 9.15 us
  blocking collectives: 13.1 us -> 12.7 us
    unnamed x12 -> x14, local copies, waits for them, and re-layouts: 3.43 us -> 1.78 us
    pallas_call x0 -> x1, Pallas kernels: none -> 1.43 us  [tap_matrix(): pl.pallas_call(tap_kernel, out_shape=jax.ShapeDtypeStruct((2 * SPAN, CHUN...]
    ppermute x8, waiting for transfers between devices: 2.46 us -> 3.25 us  [swap(): return lax.ppermute(values, 'blk', [(i, i ^ offset) for i in range(count)])]
    all_to_all x1, blocking collectives: 13.1 us -> 12.7 us  [body(): lax.all_to_all(image, 'blk', split_axis=0, concat_axis=0, tiled=True)]
    ppermute x8, starting transfers between devices: 9.58 us -> 9.15 us  [swap(): return lax.ppermute(values, 'blk', [(i, i ^ offset) for i in range(count)])]
    pallas_call x1, Pallas kernels: 1.16 us -> 0.74 us  [slit_image(): pl.pallas_call(functools.partial(image_kernel, offsets=offsets), out_shap...]
  transfers between devices with their start and end apart: 8 -> 8, of which waited for: 3 -> 3; matrix products, arithmetic and copies ran while one was open for 0% -> 0% of each run, Pallas kernels for 12% -> 16%
where the time goes in v5:
time: 35.6 us; the launch traced here: 35.3 us
  blocking collectives  12.7 us (36%)
  starting transfers between devices  9.15 us (26%)
  Pallas kernels  6.49 us (18%)
  waiting for transfers between devices  3.25 us (9%)
  local copies, waits for them, and re-layouts  1.93 us (5%)
  matrix products  0.91 us (3%)
  other arithmetic  0.79 us (2%)
    all_to_all x1, blocking collectives, body(): lax.all_to_all(image, 'blk', split_axis=0, concat_axis=0, tiled=True)  12.7 us
    ppermute x8, starting transfers between devices, swap(): return lax.ppermute(values, 'blk', [(i, i ^ offset) for i in range(count)])  9.15 us
    pallas_call x2, Pallas kernels, emission_call(): pl.pallas_call(kernel, out_shape=out_shape, in_specs=[VMEM] * len(operand...  3.65 us
    ppermute x8, waiting for transfers between devices, swap(): return lax.ppermute(values, 'blk', [(i, i ^ offset) for i in range(count)])  3.25 us
    unnamed x14, local copies, waits for them, and re-layouts  1.78 us
    pallas_call x1, Pallas kernels, tap_matrix(): pl.pallas_call(tap_kernel, out_shape=jax.ShapeDtypeStruct((2 * SPAN, CHUN...  1.43 us
    dot_general x1, matrix products, body(): lax.dot_general(onehot, pop_cells, CONTRACT_LAST, preferred_element_type=...  0.91 us
    reshape x1, other arithmetic, join(): return jnp.transpose(image, (1, 0, 2)).reshape(CELL_DEV, count * outputs)  0.77 us
  transfers between devices with their start and end apart: 8, of which 3 were waited for; matrix products, arithmetic and copies ran while one was open for 0% of the time, Pallas kernels for 16%

profile of v5, /device:TPU:0, one launch (start us, length us, event | category | flops | bytes accessed | tf_op | source)
XLA Modules:
  0.0 35.3 jit_solution(10725358991759646236)
XLA Ops:
  0.0 0.9 %copy-done = bf16[128,512]{1,0:T(8,128)(2,1)S(1)} copy-done((bf16[128,512]{1,0:T(8,128)(2,1)S(1)}, bf16[128,512]{1,0:T(8,128)(2,1)}, u32[]{:S(2)}) %copy-start) | copy-done | bytes 131096
  0.9 0.9 %constant_dynamic-update-slice_fusion.6 = (bf16[256,640]{1,0:T(8,128)(2,1)S(1)}, bf16[256,128]{1,0:T(8,128)(2,1)S(1)}) fusion(bf16[128,512]{1,0:T(8,128)(2,1)S(1)} %copy-done, s32[512]{0:T(512)} %param.7), kind=kOutput, calls=%fused_computation.20 | convolution fusion | flops 33718272 | bytes 264192 | tf_op jit(solution)/shard_map/dot_general | solution.py:246
  1.8 3.1 %collective-permute-start = (bf16[256,128]{1,0:T(8,128)(2,1)S(1)}, bf16[256,128]{1,0:T(8,128)(2,1)S(1)}, u32[]{:S(2)}, u32[]{:S(2)}) collective-permute-start(bf16[256,128]{1,0:T(8,128)(2,1)S(1)} %get-tuple-element.34), channel_id=1, source_target_pairs={{0,4},{1,5},{2,6},{3,7},{4,0},{5,1},{6,2},{7,3},{8,12},{9,13},{10,... | collective-permute-start | bytes 196616 | tf_op jit(solution)/shard_map/ppermute | solution.py:234
  4.9 2.6 %collective-permute-start.1 = (bf16[256,128]{1,0:T(8,128)(2,1)S(1)}, bf16[256,128]{1,0:T(8,128)(2,1)S(1)}, u32[]{:S(2)}, u32[]{:S(2)}) collective-permute-start(bf16[256,128]{1,0:T(8,128)(2,1)S(1)} %get-tuple-element.34), channel_id=1, source_target_pairs={{0,8},{1,9},{2,10},{3,11},{4,12},{5,13},{6,14},{7,15},{8,0},{9,1},... | collective-permute-start | bytes 196616 | tf_op jit(solution)/shard_map/ppermute | solution.py:234
  7.5 1.7 %collective-permute-start.3 = (bf16[256,128]{1,0:T(8,128)(2,1)S(1)}, bf16[256,128]{1,0:T(8,128)(2,1)S(1)}, u32[]{:S(2)}, u32[]{:S(2)}) collective-permute-start(bf16[256,128]{1,0:T(8,128)(2,1)S(1)} %get-tuple-element.34), channel_id=1, source_target_pairs={{0,2},{1,3},{2,0},{3,1},{4,6},{5,7},{6,4},{7,5},{8,10},{9,11},{10,... | collective-permute-start | bytes 196616 | tf_op jit(solution)/shard_map/ppermute | solution.py:234
  9.2 1.4 %taps.1.taps_ref = bf16[96,256]{1,0:T(8,128)(2,1)} custom-call(f32[1,129]{1,0:T(1,128)} %bitcast.16), custom_call_target="tpu_custom_call" | custom-call | flops 4294967296 | bytes 65536 | tf_op jit(solution)/shard_map/taps/pallas_call | solution.py:48
  10.7 0.8 %copy-done.3 = bf16[96,256]{1,0:T(8,128)(2,1)S(1)} copy-done((bf16[96,256]{1,0:T(8,128)(2,1)S(1)}, bf16[96,256]{1,0:T(8,128)(2,1)}, u32[]{:S(2)}) %copy-start.3) | copy-done | bytes 49176
  11.5 1.0 %emission.2.given_ref = f32[144,2048]{1,0:T(8,128)S(1)} custom-call(s32[256,128]{1,0:T(8,128)S(1)} %bitcast.11, f32[256,128]{1,0:T(8,128)S(1)} %bitcast.13, bf16[96,256]{1,0:T(8,128)(2,1)S(1)} %copy-done.3), custom_call_target="tpu_custom_call" | custom-call | flops 33554432 | bytes 65536 | tf_op jit(solution)/shard_map/emission/pallas_call | solution.py:144
  12.5 0.0 collective-permute-done
  12.5 0.0 collective-permute-done.1
  12.5 1.1 %collective-permute-done.2 = bf16[256,128]{1,0:T(8,128)(2,1)S(1)} collective-permute-done((bf16[256,128]{1,0:T(8,128)(2,1)S(1)}, bf16[256,128]{1,0:T(8,128)(2,1)S(1)}, u32[]{:S(2)}, u32[]{:S(2)}) %collective-permute-start.2) | collective-permute-done | bytes 65568 | tf_op jit(solution)/shard_map/ppermute | solution.py:234
  13.6 0.0 collective-permute-done.3
  13.6 1.6 %collective-permute-start.4 = (bf16[256,256]{1,0:T(8,128)(2,1)S(1)}, bf16[256,256]{1,0:T(8,128)(2,1)S(1)}, u32[]{:S(2)}, u32[]{:S(2)}) collective-permute-start(bf16[256,256]{1,0:T(8,128)(2,1)S(1)} %pad_maximum_fusion), channel_id=1, source_target_pairs={{0,2},{1,3},{2,0},{3,1},{4,6},{5,7},{6,4},{7,5},{8,10},{9,11},{10,... | collective-permute-start | bytes 393224 | tf_op jit(solution)/shard_map/ppermute | solution.py:234
  15.3 0.1 collective-permute-start.7
  15.4 2.6 %emission.3.terms_ref = bf16[288,2048]{1,0:T(8,128)(2,1)S(1)} custom-call(s32[256,128]{1,0:T(8,128)S(1)} %bitcast.12, f32[256,128]{1,0:T(8,128)S(1)} %bitcast.14, bf16[96,256]{1,0:T(8,128)(2,1)S(1)} %copy-done.3, f32[144,2048]{1,0:T(8,128)S(1)} %emission.2.given_ref), custom_call_target="tpu_custom_call" | custom-call | flops 100663296 | bytes 196608 | tf_op jit(solution)/shard_map/emission/pallas_call | solution.py:144
  18.0 1.4 %collective-permute-done.5 = bf16[256,128]{1,0:T(8,128)(2,1)S(1)} collective-permute-done((bf16[256,128]{1,0:T(8,128)(2,1)S(1)}, bf16[256,128]{1,0:T(8,128)(2,1)S(1)}, u32[]{:S(2)}, u32[]{:S(2)}) %collective-permute-start.5) | collective-permute-done | bytes 65568 | tf_op jit(solution)/shard_map/ppermute | solution.py:234
  19.5 0.0 copy-start.4
  19.5 0.1 collective-permute-start.6
  19.6 0.7 %early.1.given_ref = f32[256,288]{1,0:T(8,128)S(1)} custom-call(bf16[288,2048]{1,0:T(8,128)(2,1)S(1)} %emission.3.terms_ref, bf16[256,640]{1,0:T(8,128)(2,1)S(1)} %constant_dynamic-update-slice_fusion.2.refs_0_, bf16[256,640]{1,0:T(8,128)(2,1)S(1)} %collective-permute-done.7.refs_1_, bf16[256,384]{1,0:T(8,128)(2,1)S(1)} %constant_dynamic-update-slice_fusion.refs_2_), custom_call_target="tpu_custom_call" | custom-call | flops 805306368 | bytes 1048576 | tf_op jit(solution)/shard_map/early/pallas_call | solution.py:210
  20.3 0.7 %collective-permute-done.6.refs_0_ = bf16[256,384]{1,0:T(8,128)(2,1)S(1)} collective-permute-done((bf16[256,384]{1,0:T(8,128)(2,1)S(1)}, bf16[256,384]{1,0:T(8,128)(2,1)S(1)}, u32[]{:S(2)}, u32[]{:S(2)}) %collective-permute-start.6) | collective-permute-done | bytes 196640 | tf_op jit(solution)/shard_map/ppermute | solution.py:234
  21.0 0.7 %image.1 = f32[16,24,128]{2,1,0:T(8,128)S(1)} custom-call(f32[1,9]{1,0:T(1,128)S(1)} %bitcast.15, bf16[288,2048]{1,0:T(8,128)(2,1)S(1)} %emission.3.terms_ref, f32[256,288]{1,0:T(8,128)S(1)} %early.1.given_ref, bf16[256,384]{1,0:T(8,128)(2,1)S(1)} %collective-permute-done.6.refs_0_), custom_call_target="tpu_custom_call" | custom-call | flops 268435456 | bytes 1048576 | tf_op jit(solution)/shard_map/image/pallas_call | solution.py:222
  21.8 12.7 %all_to_all.5 = f32[16,24,128]{2,1,0:T(8,128)S(1)} all-to-all(f32[16,24,128]{2,1,0:T(8,128)S(1)} %image.1), channel_id=1, replica_groups=mesh['groups'=2,'blk'=16] {'blk'}, dimensions={0} | all-to-all | bytes 393216 | tf_op jit(solution)/shard_map/all_to_all | solution.py:280
  34.4 0.1 fusion.4
  34.5 0.8 %copy_bitcast_fusion = f32[16,2048]{1,0:T(8,128)} fusion(f32[15,8,8]{2,1,0:T(8,128)S(1)} %get-tuple-element.30, f32[15,8,8]{2,1,0:T(8,128)S(1)} %get-tuple-element.31, f32[15,8,8]{2,1,0:T(8,128)S(1)} %get-tuple-element.32, f32[15,8,8]{2,1,0:T(8,128)S(1)} %get-tuple-element.29, f32[16,24,128]{2,1,0:T(8,128)S(1)} %all_to_all.5), kind=kLoop, calls=%fused_computation.3 | loop fusion | flops 589824 | bytes 507904 | tf_op jit(solution)/shard_map/reshape | solution.py:206
  (18 shorter events, 0.1 us)
Async XLA Ops:
  0.0 0.9 %copy-start = (bf16[128,512]{1,0:T(8,128)(2,1)S(1)}, bf16[128,512]{1,0:T(8,128)(2,1)}, u32[]{:S(2)}) copy-start(bf16[128,512]{1,0:T(8,128)(2,1)} %param.6) | copy-start | bytes 393220
  1.8 10.7 %collective-permute-start = (bf16[256,128]{1,0:T(8,128)(2,1)S(1)}, bf16[256,128]{1,0:T(8,128)(2,1)S(1)}, u32[]{:S(2)}, u32[]{:S(2)}) collective-permute-start(bf16[256,128]{1,0:T(8,128)(2,1)S(1)} %get-tuple-element.34), channel_id=1, source_target_pairs={{0,4},{1,5},{2,6},{3,7},{4,0},{5,1},{6,2},{7,3},{8,12},{9,13},{10,... | collective-permute-start | bytes 196616 | tf_op jit(solution)/shard_map/ppermute | solution.py:234
  4.9 7.6 %collective-permute-start.1 = (bf16[256,128]{1,0:T(8,128)(2,1)S(1)}, bf16[256,128]{1,0:T(8,128)(2,1)S(1)}, u32[]{:S(2)}, u32[]{:S(2)}) collective-permute-start(bf16[256,128]{1,0:T(8,128)(2,1)S(1)} %get-tuple-element.34), channel_id=1, source_target_pairs={{0,8},{1,9},{2,10},{3,11},{4,12},{5,13},{6,14},{7,15},{8,0},{9,1},... | collective-permute-start | bytes 196616 | tf_op jit(solution)/shard_map/ppermute | solution.py:234
  7.5 6.1 %collective-permute-start.2 = (bf16[256,128]{1,0:T(8,128)(2,1)S(1)}, bf16[256,128]{1,0:T(8,128)(2,1)S(1)}, u32[]{:S(2)}, u32[]{:S(2)}) collective-permute-start(bf16[256,128]{1,0:T(8,128)(2,1)S(1)} %get-tuple-element.34), channel_id=1, source_target_pairs={{0,12},{1,13},{2,14},{3,15},{4,8},{5,9},{6,10},{7,11},{8,4},{9,5},... | collective-permute-start | bytes 196616 | tf_op jit(solution)/shard_map/ppermute | solution.py:234
  7.5 6.1 %collective-permute-start.3 = (bf16[256,128]{1,0:T(8,128)(2,1)S(1)}, bf16[256,128]{1,0:T(8,128)(2,1)S(1)}, u32[]{:S(2)}, u32[]{:S(2)}) collective-permute-start(bf16[256,128]{1,0:T(8,128)(2,1)S(1)} %get-tuple-element.34), channel_id=1, source_target_pairs={{0,2},{1,3},{2,0},{3,1},{4,6},{5,7},{6,4},{7,5},{8,10},{9,11},{10,... | collective-permute-start | bytes 196616 | tf_op jit(solution)/shard_map/ppermute | solution.py:234
  9.2 1.4 %copy-start.1 = (s32[32768]{0:T(1024)S(1)}, s32[32768]{0:T(1024)}, u32[]{:S(2)}) copy-start(s32[32768]{0:T(1024)} %param.8) | copy-start | bytes 393220
  9.2 1.4 %copy-start.2 = (f32[32768]{0:T(1024)S(1)}, f32[32768]{0:T(1024)}, u32[]{:S(2)}) copy-start(f32[32768]{0:T(1024)} %param.9) | copy-start | bytes 393220
  10.7 0.8 %copy-start.3 = (bf16[96,256]{1,0:T(8,128)(2,1)S(1)}, bf16[96,256]{1,0:T(8,128)(2,1)}, u32[]{:S(2)}) copy-start(bf16[96,256]{1,0:T(8,128)(2,1)} %taps.1.taps_ref) | copy-start | bytes 147460
  13.6 5.9 %collective-permute-start.4 = (bf16[256,256]{1,0:T(8,128)(2,1)S(1)}, bf16[256,256]{1,0:T(8,128)(2,1)S(1)}, u32[]{:S(2)}, u32[]{:S(2)}) collective-permute-start(bf16[256,256]{1,0:T(8,128)(2,1)S(1)} %pad_maximum_fusion), channel_id=1, source_target_pairs={{0,2},{1,3},{2,0},{3,1},{4,6},{5,7},{6,4},{7,5},{8,10},{9,11},{10,... | collective-permute-start | bytes 393224 | tf_op jit(solution)/shard_map/ppermute | solution.py:234
  15.2 4.3 %collective-permute-start.5 = (bf16[256,128]{1,0:T(8,128)(2,1)S(1)}, bf16[256,128]{1,0:T(8,128)(2,1)S(1)}, u32[]{:S(2)}, u32[]{:S(2)}) collective-permute-start(bf16[256,128]{1,0:T(8,128)(2,1)S(1)} %collective-permute-done.3), channel_id=1, source_target_pairs={{0,4},{1,5},{2,6},{3,7},{4,0},{5,1},{6,2},{7,3},{8,12},{9,13},{10,... | collective-permute-start | bytes 196616 | tf_op jit(solution)/shard_map/ppermute | solution.py:234
  15.3 4.3 %collective-permute-start.7 = (bf16[256,640]{1,0:T(8,128)(2,1)S(1)}, bf16[256,640]{1,0:T(8,128)(2,1)S(1)}, u32[]{:S(2)}, u32[]{:S(2)}) collective-permute-start(bf16[256,640]{1,0:T(8,128)(2,1)S(1)} %constant_dynamic-update-slice_fusion.2.refs_0_), channel_id=1, source_target_pairs={{0,1},{1,0},{2,3},{3,2},{4,5},{5,4},{6,7},{7,6},{8,9},{9,8},{10,11... | collective-permute-start | bytes 983048 | tf_op jit(solution)/shard_map/ppermute | solution.py:234
  19.5 1.5 %copy-start.4 = (f32[9]{0:T(128)S(1)}, f32[9]{0:T(128)}, u32[]{:S(2)}) copy-start(f32[9]{0:T(128)} %param.11) | copy-start | bytes 112
  19.5 1.5 %collective-permute-start.6 = (bf16[256,384]{1,0:T(8,128)(2,1)S(1)}, bf16[256,384]{1,0:T(8,128)(2,1)S(1)}, u32[]{:S(2)}, u32[]{:S(2)}) collective-permute-start(bf16[256,384]{1,0:T(8,128)(2,1)S(1)} %constant_dynamic-update-slice_fusion.refs_2_), channel_id=1, source_target_pairs={{0,1},{1,0},{2,3},{3,2},{4,5},{5,4},{6,7},{7,6},{8,9},{9,8},{10,11... | collective-permute-start | bytes 589832 | tf_op jit(solution)/shard_map/ppermute | solution.py:234

commit v6 on v5

--- a/solution.py
+++ b/solution.py
@@ -50,6 +50,7 @@
         out_shape=jax.ShapeDtypeStruct((2 * SPAN, CHUNK), BF16),
         in_specs=[VMEM],
         scratch_shapes=[pltpu.VMEM((8, TAP_WIDTH), F32)],
+        compiler_params=pltpu.CompilerParams(vmem_limit_bytes=VMEM_LIMIT),
         cost_estimate=pl.CostEstimate(flops=TAP_FLOPS, bytes_accessed=1 << 16, transcendentals=0),
         name="taps",
     )(wave)

time: 35.6 us -> 35.2 us (0.989)
  Pallas kernels: 6.49 us -> 5.14 us
  local copies, waits for them, and re-layouts: 1.93 us -> 2.68 us
  waiting for transfers between devices: 3.25 us -> 3.85 us
  blocking collectives: 12.7 us -> 12.3 us
    pallas_call x1, Pallas kernels: 1.43 us -> 0.08 us  [tap_matrix(): pl.pallas_call(tap_kernel, out_shape=jax.ShapeDtypeStruct((2 * SPAN, CHUN...]
    unnamed x14, local copies, waits for them, and re-layouts: 1.78 us -> 2.54 us
    ppermute x8, waiting for transfers between devices: 3.25 us -> 3.85 us  [swap(): return lax.ppermute(values, 'blk', [(i, i ^ offset) for i in range(count)])]
  transfers between devices with their start and end apart: 8 -> 8, of which waited for: 3 -> 4; matrix products, arithmetic and copies ran while one was open for 0% -> 0% of each run, Pallas kernels for 16% -> 13%
where the time goes in v6:
time: 35.2 us; the launch traced here: 34.9 us
  blocking collectives  12.3 us (35%)
  starting transfers between devices  9.15 us (26%)
  Pallas kernels  5.14 us (15%)
  waiting for transfers between devices  3.85 us (11%)
  local copies, waits for them, and re-layouts  2.68 us (8%)
  matrix products  0.91 us (3%)
  other arithmetic  0.79 us (2%)
    all_to_all x1, blocking collectives, body(): lax.all_to_all(image, 'blk', split_axis=0, concat_axis=0, tiled=True)  12.3 us
    ppermute x8, starting transfers between devices, swap(): return lax.ppermute(values, 'blk', [(i, i ^ offset) for i in range(count)])  9.15 us
    ppermute x8, waiting for transfers between devices, swap(): return lax.ppermute(values, 'blk', [(i, i ^ offset) for i in range(count)])  3.85 us
    pallas_call x2, Pallas kernels, emission_call(): pl.pallas_call(kernel, out_shape=out_shape, in_specs=[VMEM] * len(operand...  3.65 us
    unnamed x14, local copies, waits for them, and re-layouts  2.54 us
    dot_general x1, matrix products, body(): lax.dot_general(onehot, pop_cells, CONTRACT_LAST, preferred_element_type=...  0.91 us
    reshape x1, other arithmetic, join(): return jnp.transpose(image, (1, 0, 2)).reshape(CELL_DEV, count * outputs)  0.77 us
    pallas_call x1, Pallas kernels, slit_image(): pl.pallas_call(functools.partial(image_kernel, offsets=offsets), out_shap...  0.74 us
  transfers between devices with their start and end apart: 8, of which 4 were waited for; matrix products, arithmetic and copies ran while one was open for 0% of the time, Pallas kernels for 13%

profile of v6, /device:TPU:0, one launch (start us, length us, event | category | flops | bytes accessed | tf_op | source)
XLA Modules:
  0.0 34.9 jit_solution(13655545006702800534)
XLA Ops:
  0.0 0.9 %copy-done = bf16[128,512]{1,0:T(8,128)(2,1)S(1)} copy-done((bf16[128,512]{1,0:T(8,128)(2,1)S(1)}, bf16[128,512]{1,0:T(8,128)(2,1)}, u32[]{:S(2)}) %copy-start) | copy-done | bytes 131096
  0.9 0.9 %constant_dynamic-update-slice_fusion.6 = (bf16[256,640]{1,0:T(8,128)(2,1)S(1)}, bf16[256,128]{1,0:T(8,128)(2,1)S(1)}) fusion(bf16[128,512]{1,0:T(8,128)(2,1)S(1)} %copy-done, s32[512]{0:T(512)} %param.7), kind=kOutput, calls=%fused_computation.20 | convolution fusion | flops 33718272 | bytes 264192 | tf_op jit(solution)/shard_map/dot_general | solution.py:247
  1.8 3.1 %collective-permute-start = (bf16[256,128]{1,0:T(8,128)(2,1)S(1)}, bf16[256,128]{1,0:T(8,128)(2,1)S(1)}, u32[]{:S(2)}, u32[]{:S(2)}) collective-permute-start(bf16[256,128]{1,0:T(8,128)(2,1)S(1)} %get-tuple-element.34), channel_id=1, source_target_pairs={{0,4},{1,5},{2,6},{3,7},{4,0},{5,1},{6,2},{7,3},{8,12},{9,13},{10,... | collective-permute-start | bytes 196616 | tf_op jit(solution)/shard_map/ppermute | solution.py:235
  4.9 2.6 %collective-permute-start.1 = (bf16[256,128]{1,0:T(8,128)(2,1)S(1)}, bf16[256,128]{1,0:T(8,128)(2,1)S(1)}, u32[]{:S(2)}, u32[]{:S(2)}) collective-permute-start(bf16[256,128]{1,0:T(8,128)(2,1)S(1)} %get-tuple-element.34), channel_id=1, source_target_pairs={{0,8},{1,9},{2,10},{3,11},{4,12},{5,13},{6,14},{7,15},{8,0},{9,1},... | collective-permute-start | bytes 196616 | tf_op jit(solution)/shard_map/ppermute | solution.py:235
  7.5 1.7 %collective-permute-start.3 = (bf16[256,128]{1,0:T(8,128)(2,1)S(1)}, bf16[256,128]{1,0:T(8,128)(2,1)S(1)}, u32[]{:S(2)}, u32[]{:S(2)}) collective-permute-start(bf16[256,128]{1,0:T(8,128)(2,1)S(1)} %get-tuple-element.34), channel_id=1, source_target_pairs={{0,2},{1,3},{2,0},{3,1},{4,6},{5,7},{6,4},{7,5},{8,10},{9,11},{10,... | collective-permute-start | bytes 196616 | tf_op jit(solution)/shard_map/ppermute | solution.py:235
  9.2 0.7 %copy-done.4 = f32[129]{0:T(256)S(1)} copy-done((f32[129]{0:T(256)S(1)}, f32[129]{0:T(256)}, u32[]{:S(2)}) %copy-start.4) | copy-done | bytes 540
  9.9 0.1 taps.1.taps_ref
  10.0 0.8 %copy-done.1 = s32[32768]{0:T(1024)S(1)} copy-done((s32[32768]{0:T(1024)S(1)}, s32[32768]{0:T(1024)}, u32[]{:S(2)}) %copy-start.1) | copy-done | bytes 131096
  10.8 0.1 copy-done.2
  10.9 1.0 %emission.2.given_ref = f32[144,2048]{1,0:T(8,128)S(1)} custom-call(s32[256,128]{1,0:T(8,128)S(1)} %bitcast.11, f32[256,128]{1,0:T(8,128)S(1)} %bitcast.13, bf16[96,256]{1,0:T(8,128)(2,1)S(1)} %taps.1.taps_ref), custom_call_target="tpu_custom_call" | custom-call | flops 33554432 | bytes 65536 | tf_op jit(solution)/shard_map/emission/pallas_call | solution.py:145
  11.9 0.3 collective-permute-done.1
  12.2 1.4 %collective-permute-done.2 = bf16[256,128]{1,0:T(8,128)(2,1)S(1)} collective-permute-done((bf16[256,128]{1,0:T(8,128)(2,1)S(1)}, bf16[256,128]{1,0:T(8,128)(2,1)S(1)}, u32[]{:S(2)}, u32[]{:S(2)}) %collective-permute-start.2) | collective-permute-done | bytes 65568 | tf_op jit(solution)/shard_map/ppermute | solution.py:235
  13.6 1.6 %collective-permute-start.4 = (bf16[256,256]{1,0:T(8,128)(2,1)S(1)}, bf16[256,256]{1,0:T(8,128)(2,1)S(1)}, u32[]{:S(2)}, u32[]{:S(2)}) collective-permute-start(bf16[256,256]{1,0:T(8,128)(2,1)S(1)} %pad_maximum_fusion), channel_id=1, source_target_pairs={{0,2},{1,3},{2,0},{3,1},{4,6},{5,7},{6,4},{7,5},{8,10},{9,11},{10,... | collective-permute-start | bytes 393224 | tf_op jit(solution)/shard_map/ppermute | solution.py:235
  15.3 0.1 collective-permute-start.7
  15.4 2.6 %emission.3.terms_ref = bf16[288,2048]{1,0:T(8,128)(2,1)S(1)} custom-call(s32[256,128]{1,0:T(8,128)S(1)} %bitcast.12, f32[256,128]{1,0:T(8,128)S(1)} %bitcast.14, bf16[96,256]{1,0:T(8,128)(2,1)S(1)} %taps.1.taps_ref, f32[144,2048]{1,0:T(8,128)S(1)} %emission.2.given_ref), custom_call_target="tpu_custom_call" | custom-call | flops 100663296 | bytes 196608 | tf_op jit(solution)/shard_map/emission/pallas_call | solution.py:145
  18.0 1.4 %collective-permute-done.5 = bf16[256,128]{1,0:T(8,128)(2,1)S(1)} collective-permute-done((bf16[256,128]{1,0:T(8,128)(2,1)S(1)}, bf16[256,128]{1,0:T(8,128)(2,1)S(1)}, u32[]{:S(2)}, u32[]{:S(2)}) %collective-permute-start.5) | collective-permute-done | bytes 65568 | tf_op jit(solution)/shard_map/ppermute | solution.py:235
  19.5 0.0 copy-start.3
  19.5 0.1 collective-permute-start.6
  19.6 0.7 %early.1.given_ref = f32[256,288]{1,0:T(8,128)S(1)} custom-call(bf16[288,2048]{1,0:T(8,128)(2,1)S(1)} %emission.3.terms_ref, bf16[256,640]{1,0:T(8,128)(2,1)S(1)} %constant_dynamic-update-slice_fusion.2.refs_0_, bf16[256,640]{1,0:T(8,128)(2,1)S(1)} %collective-permute-done.7.refs_1_, bf16[256,384]{1,0:T(8,128)(2,1)S(1)} %constant_dynamic-update-slice_fusion.refs_2_), custom_call_target="tpu_custom_call" | custom-call | flops 805306368 | bytes 1048576 | tf_op jit(solution)/shard_map/early/pallas_call | solution.py:211
  20.3 0.7 %collective-permute-done.6.refs_0_ = bf16[256,384]{1,0:T(8,128)(2,1)S(1)} collective-permute-done((bf16[256,384]{1,0:T(8,128)(2,1)S(1)}, bf16[256,384]{1,0:T(8,128)(2,1)S(1)}, u32[]{:S(2)}, u32[]{:S(2)}) %collective-permute-start.6) | collective-permute-done | bytes 196640 | tf_op jit(solution)/shard_map/ppermute | solution.py:235
  21.0 0.7 %image.1 = f32[16,24,128]{2,1,0:T(8,128)S(1)} custom-call(f32[1,9]{1,0:T(1,128)S(1)} %bitcast.15, bf16[288,2048]{1,0:T(8,128)(2,1)S(1)} %emission.3.terms_ref, f32[256,288]{1,0:T(8,128)S(1)} %early.1.given_ref, bf16[256,384]{1,0:T(8,128)(2,1)S(1)} %collective-permute-done.6.refs_0_), custom_call_target="tpu_custom_call" | custom-call | flops 268435456 | bytes 1048576 | tf_op jit(solution)/shard_map/image/pallas_call | solution.py:223
  21.8 12.3 %all_to_all.5 = f32[16,24,128]{2,1,0:T(8,128)S(1)} all-to-all(f32[16,24,128]{2,1,0:T(8,128)S(1)} %image.1), channel_id=1, replica_groups=mesh['groups'=2,'blk'=16] {'blk'}, dimensions={0} | all-to-all | bytes 393216 | tf_op jit(solution)/shard_map/all_to_all | solution.py:281
  34.1 0.1 fusion.4
  34.2 0.8 %copy_bitcast_fusion = f32[16,2048]{1,0:T(8,128)} fusion(f32[15,8,8]{2,1,0:T(8,128)S(1)} %get-tuple-element.30, f32[15,8,8]{2,1,0:T(8,128)S(1)} %get-tuple-element.31, f32[15,8,8]{2,1,0:T(8,128)S(1)} %get-tuple-element.32, f32[15,8,8]{2,1,0:T(8,128)S(1)} %get-tuple-element.29, f32[16,24,128]{2,1,0:T(8,128)S(1)} %all_to_all.5), kind=kLoop, calls=%fused_computation.3 | loop fusion | flops 589824 | bytes 507904 | tf_op jit(solution)/shard_map/reshape | solution.py:207
  (18 shorter events, 0.1 us)
Async XLA Ops:
  0.0 0.9 %copy-start = (bf16[128,512]{1,0:T(8,128)(2,1)S(1)}, bf16[128,512]{1,0:T(8,128)(2,1)}, u32[]{:S(2)}) copy-start(bf16[128,512]{1,0:T(8,128)(2,1)} %param.6) | copy-start | bytes 393220
  1.8 10.1 %collective-permute-start = (bf16[256,128]{1,0:T(8,128)(2,1)S(1)}, bf16[256,128]{1,0:T(8,128)(2,1)S(1)}, u32[]{:S(2)}, u32[]{:S(2)}) collective-permute-start(bf16[256,128]{1,0:T(8,128)(2,1)S(1)} %get-tuple-element.34), channel_id=1, source_target_pairs={{0,4},{1,5},{2,6},{3,7},{4,0},{5,1},{6,2},{7,3},{8,12},{9,13},{10,... | collective-permute-start | bytes 196616 | tf_op jit(solution)/shard_map/ppermute | solution.py:235
  4.9 7.3 %collective-permute-start.1 = (bf16[256,128]{1,0:T(8,128)(2,1)S(1)}, bf16[256,128]{1,0:T(8,128)(2,1)S(1)}, u32[]{:S(2)}, u32[]{:S(2)}) collective-permute-start(bf16[256,128]{1,0:T(8,128)(2,1)S(1)} %get-tuple-element.34), channel_id=1, source_target_pairs={{0,8},{1,9},{2,10},{3,11},{4,12},{5,13},{6,14},{7,15},{8,0},{9,1},... | collective-permute-start | bytes 196616 | tf_op jit(solution)/shard_map/ppermute | solution.py:235
  7.5 6.1 %collective-permute-start.2 = (bf16[256,128]{1,0:T(8,128)(2,1)S(1)}, bf16[256,128]{1,0:T(8,128)(2,1)S(1)}, u32[]{:S(2)}, u32[]{:S(2)}) collective-permute-start(bf16[256,128]{1,0:T(8,128)(2,1)S(1)} %get-tuple-element.34), channel_id=1, source_target_pairs={{0,12},{1,13},{2,14},{3,15},{4,8},{5,9},{6,10},{7,11},{8,4},{9,5},... | collective-permute-start | bytes 196616 | tf_op jit(solution)/shard_map/ppermute | solution.py:235
  7.5 6.1 %collective-permute-start.3 = (bf16[256,128]{1,0:T(8,128)(2,1)S(1)}, bf16[256,128]{1,0:T(8,128)(2,1)S(1)}, u32[]{:S(2)}, u32[]{:S(2)}) collective-permute-start(bf16[256,128]{1,0:T(8,128)(2,1)S(1)} %get-tuple-element.34), channel_id=1, source_target_pairs={{0,2},{1,3},{2,0},{3,1},{4,6},{5,7},{6,4},{7,5},{8,10},{9,11},{10,... | collective-permute-start | bytes 196616 | tf_op jit(solution)/shard_map/ppermute | solution.py:235
  9.2 0.7 %copy-start.4 = (f32[129]{0:T(256)S(1)}, f32[129]{0:T(256)}, u32[]{:S(2)}) copy-start(f32[129]{0:T(256)} %param.10) | copy-start | bytes 1552
  9.9 0.9 %copy-start.1 = (s32[32768]{0:T(1024)S(1)}, s32[32768]{0:T(1024)}, u32[]{:S(2)}) copy-start(s32[32768]{0:T(1024)} %param.8) | copy-start | bytes 393220
  9.9 1.0 %copy-start.2 = (f32[32768]{0:T(1024)S(1)}, f32[32768]{0:T(1024)}, u32[]{:S(2)}) copy-start(f32[32768]{0:T(1024)} %param.9) | copy-start | bytes 393220
  13.6 5.9 %collective-permute-start.4 = (bf16[256,256]{1,0:T(8,128)(2,1)S(1)}, bf16[256,256]{1,0:T(8,128)(2,1)S(1)}, u32[]{:S(2)}, u32[]{:S(2)}) collective-permute-start(bf16[256,256]{1,0:T(8,128)(2,1)S(1)} %pad_maximum_fusion), channel_id=1, source_target_pairs={{0,2},{1,3},{2,0},{3,1},{4,6},{5,7},{6,4},{7,5},{8,10},{9,11},{10,... | collective-permute-start | bytes 393224 | tf_op jit(solution)/shard_map/ppermute | solution.py:235
  15.2 4.3 %collective-permute-start.5 = (bf16[256,128]{1,0:T(8,128)(2,1)S(1)}, bf16[256,128]{1,0:T(8,128)(2,1)S(1)}, u32[]{:S(2)}, u32[]{:S(2)}) collective-permute-start(bf16[256,128]{1,0:T(8,128)(2,1)S(1)} %collective-permute-done.3), channel_id=1, source_target_pairs={{0,4},{1,5},{2,6},{3,7},{4,0},{5,1},{6,2},{7,3},{8,12},{9,13},{10,... | collective-permute-start | bytes 196616 | tf_op jit(solution)/shard_map/ppermute | solution.py:235
  15.3 4.3 %collective-permute-start.7 = (bf16[256,640]{1,0:T(8,128)(2,1)S(1)}, bf16[256,640]{1,0:T(8,128)(2,1)S(1)}, u32[]{:S(2)}, u32[]{:S(2)}) collective-permute-start(bf16[256,640]{1,0:T(8,128)(2,1)S(1)} %constant_dynamic-update-slice_fusion.2.refs_0_), channel_id=1, source_target_pairs={{0,1},{1,0},{2,3},{3,2},{4,5},{5,4},{6,7},{7,6},{8,9},{9,8},{10,11... | collective-permute-start | bytes 983048 | tf_op jit(solution)/shard_map/ppermute | solution.py:235
  19.5 1.5 %copy-start.3 = (f32[9]{0:T(128)S(1)}, f32[9]{0:T(128)}, u32[]{:S(2)}) copy-start(f32[9]{0:T(128)} %param.11) | copy-start | bytes 112
  19.5 1.5 %collective-permute-start.6 = (bf16[256,384]{1,0:T(8,128)(2,1)S(1)}, bf16[256,384]{1,0:T(8,128)(2,1)S(1)}, u32[]{:S(2)}, u32[]{:S(2)}) collective-permute-start(bf16[256,384]{1,0:T(8,128)(2,1)S(1)} %constant_dynamic-update-slice_fusion.refs_2_), channel_id=1, source_target_pairs={{0,1},{1,0},{2,3},{3,2},{4,5},{5,4},{6,7},{7,6},{8,9},{9,8},{10,11... | collective-permute-start | bytes 589832 | tf_op jit(solution)/shard_map/ppermute | solution.py:235

commit v7 on v6

--- a/solution.py
+++ b/solution.py
@@ -244,6 +244,7 @@
     hold = lax.optimization_barrier
 
     onehot = (cell_map[None, :] == jnp.arange(cells, dtype=jnp.int32)[:, None]).astype(BF16)
+    onehot = hold(onehot)
     pop = lax.dot_general(onehot, pop_cells, CONTRACT_LAST, preferred_element_type=F32).astype(BF16)
     if count > HIGH:
         sets = [list(range(i, count, HIGH)) for i in range(HIGH)]

time: 35.2 us -> 34.5 us (0.980)
  local copies, waits for them, and re-layouts: 2.68 us -> 1.92 us
  other arithmetic: 0.79 us -> 1.55 us
  matrix products: 0.91 us -> 0.23 us
    convert_element_type x0 -> x1, other arithmetic: none -> 0.77 us  [body(): (cell_map[None, :] == jnp.arange(cells, dtype=jnp.int32)[:, None]).astype...]
    unnamed x14, local copies, waits for them, and re-layouts: 2.54 us -> 1.78 us
    dot_general x1, matrix products: 0.91 us -> 0.23 us  [body(): lax.dot_general(onehot, pop_cells, CONTRACT_LAST, preferred_element_type=...]
where the time goes in v7:
time: 34.5 us; the launch traced here: 34.3 us
  blocking collectives  12.3 us (36%)
  starting transfers between devices  9.15 us (27%)
  Pallas kernels  5.14 us (15%)
  waiting for transfers between devices  3.84 us (11%)
  local copies, waits for them, and re-layouts  1.92 us (6%)
  other arithmetic  1.55 us (4%)
    all_to_all x1, blocking collectives, body(): lax.all_to_all(image, 'blk', split_axis=0, concat_axis=0, tiled=True)  12.3 us
    ppermute x8, starting transfers between devices, swap(): return lax.ppermute(values, 'blk', [(i, i ^ offset) for i in range(count)])  9.15 us
    ppermute x8, waiting for transfers between devices, swap(): return lax.ppermute(values, 'blk', [(i, i ^ offset) for i in range(count)])  3.84 us
    pallas_call x2, Pallas kernels, emission_call(): pl.pallas_call(kernel, out_shape=out_shape, in_specs=[VMEM] * len(operand...  3.65 us
    unnamed x14, local copies, waits for them, and re-layouts  1.78 us
    reshape x1, other arithmetic, join(): return jnp.transpose(image, (1, 0, 2)).reshape(CELL_DEV, count * outputs)  0.77 us
    convert_element_type x1, other arithmetic, body(): (cell_map[None, :] == jnp.arange(cells, dtype=jnp.int32)[:, None]).astype...  0.77 us
    pallas_call x1, Pallas kernels, slit_image(): pl.pallas_call(functools.partial(image_kernel, offsets=offsets), out_shap...  0.74 us
  transfers between devices with their start and end apart: 8, of which 4 were waited for; matrix products, arithmetic and copies ran while one was open for 0% of the time, Pallas kernels for 13%

profile of v7, /device:TPU:0, one launch (start us, length us, event | category | flops | bytes accessed | tf_op | source)
XLA Modules:
  0.0 34.3 jit_solution(11365333058556286190)
XLA Ops:
  0.0 0.8 %fusion = bf16[256,512]{1,0:T(8,128)(2,1)S(1)} fusion(s32[512]{0:T(512)} %param.7), kind=kLoop, calls=%fused_computation.2 | loop fusion | flops 262144 | bytes 264192 | tf_op jit(solution)/shard_map/convert_element_type | solution.py:246
  0.8 0.1 copy-done
  0.9 0.2 constant_dynamic-update-slice_fusion.6
  1.2 3.1 %collective-permute-start = (bf16[256,128]{1,0:T(8,128)(2,1)S(1)}, bf16[256,128]{1,0:T(8,128)(2,1)S(1)}, u32[]{:S(2)}, u32[]{:S(2)}) collective-permute-start(bf16[256,128]{1,0:T(8,128)(2,1)S(1)} %get-tuple-element.34), channel_id=1, source_target_pairs={{0,4},{1,5},{2,6},{3,7},{4,0},{5,1},{6,2},{7,3},{8,12},{9,13},{10,... | collective-permute-start | bytes 196616 | tf_op jit(solution)/shard_map/ppermute | solution.py:235
  4.2 2.6 %collective-permute-start.1 = (bf16[256,128]{1,0:T(8,128)(2,1)S(1)}, bf16[256,128]{1,0:T(8,128)(2,1)S(1)}, u32[]{:S(2)}, u32[]{:S(2)}) collective-permute-start(bf16[256,128]{1,0:T(8,128)(2,1)S(1)} %get-tuple-element.34), channel_id=1, source_target_pairs={{0,8},{1,9},{2,10},{3,11},{4,12},{5,13},{6,14},{7,15},{8,0},{9,1},... | collective-permute-start | bytes 196616 | tf_op jit(solution)/shard_map/ppermute | solution.py:235
  6.8 1.7 %collective-permute-start.3 = (bf16[256,128]{1,0:T(8,128)(2,1)S(1)}, bf16[256,128]{1,0:T(8,128)(2,1)S(1)}, u32[]{:S(2)}, u32[]{:S(2)}) collective-permute-start(bf16[256,128]{1,0:T(8,128)(2,1)S(1)} %get-tuple-element.34), channel_id=1, source_target_pairs={{0,2},{1,3},{2,0},{3,1},{4,6},{5,7},{6,4},{7,5},{8,10},{9,11},{10,... | collective-permute-start | bytes 196616 | tf_op jit(solution)/shard_map/ppermute | solution.py:235
  8.6 0.7 %copy-done.4 = f32[129]{0:T(256)S(1)} copy-done((f32[129]{0:T(256)S(1)}, f32[129]{0:T(256)}, u32[]{:S(2)}) %copy-start.4) | copy-done | bytes 540
  9.3 0.1 taps.1.taps_ref
  9.3 0.8 %copy-done.1 = s32[32768]{0:T(1024)S(1)} copy-done((s32[32768]{0:T(1024)S(1)}, s32[32768]{0:T(1024)}, u32[]{:S(2)}) %copy-start.1) | copy-done | bytes 131096
  10.2 0.1 copy-done.2
  10.2 1.0 %emission.2.given_ref = f32[144,2048]{1,0:T(8,128)S(1)} custom-call(s32[256,128]{1,0:T(8,128)S(1)} %bitcast.12, f32[256,128]{1,0:T(8,128)S(1)} %bitcast.14, bf16[96,256]{1,0:T(8,128)(2,1)S(1)} %taps.1.taps_ref), custom_call_target="tpu_custom_call" | custom-call | flops 33554432 | bytes 65536 | tf_op jit(solution)/shard_map/emission/pallas_call | solution.py:145
  11.2 0.3 collective-permute-done.1
  11.5 1.4 %collective-permute-done.2 = bf16[256,128]{1,0:T(8,128)(2,1)S(1)} collective-permute-done((bf16[256,128]{1,0:T(8,128)(2,1)S(1)}, bf16[256,128]{1,0:T(8,128)(2,1)S(1)}, u32[]{:S(2)}, u32[]{:S(2)}) %collective-permute-start.2) | collective-permute-done | bytes 65568 | tf_op jit(solution)/shard_map/ppermute | solution.py:235
  12.9 1.6 %collective-permute-start.4 = (bf16[256,256]{1,0:T(8,128)(2,1)S(1)}, bf16[256,256]{1,0:T(8,128)(2,1)S(1)}, u32[]{:S(2)}, u32[]{:S(2)}) collective-permute-start(bf16[256,256]{1,0:T(8,128)(2,1)S(1)} %pad_maximum_fusion), channel_id=1, source_target_pairs={{0,2},{1,3},{2,0},{3,1},{4,6},{5,7},{6,4},{7,5},{8,10},{9,11},{10,... | collective-permute-start | bytes 393224 | tf_op jit(solution)/shard_map/ppermute | solution.py:235
  14.6 0.1 collective-permute-start.7
  14.7 2.6 %emission.3.terms_ref = bf16[288,2048]{1,0:T(8,128)(2,1)S(1)} custom-call(s32[256,128]{1,0:T(8,128)S(1)} %bitcast.13, f32[256,128]{1,0:T(8,128)S(1)} %bitcast.15, bf16[96,256]{1,0:T(8,128)(2,1)S(1)} %taps.1.taps_ref, f32[144,2048]{1,0:T(8,128)S(1)} %emission.2.given_ref), custom_call_target="tpu_custom_call" | custom-call | flops 100663296 | bytes 196608 | tf_op jit(solution)/shard_map/emission/pallas_call | solution.py:145
  17.3 1.4 %collective-permute-done.5 = bf16[256,128]{1,0:T(8,128)(2,1)S(1)} collective-permute-done((bf16[256,128]{1,0:T(8,128)(2,1)S(1)}, bf16[256,128]{1,0:T(8,128)(2,1)S(1)}, u32[]{:S(2)}, u32[]{:S(2)}) %collective-permute-start.5) | collective-permute-done | bytes 65568 | tf_op jit(solution)/shard_map/ppermute | solution.py:235
  18.8 0.1 collective-permute-start.6
  18.9 0.7 %early.1.given_ref = f32[256,288]{1,0:T(8,128)S(1)} custom-call(bf16[288,2048]{1,0:T(8,128)(2,1)S(1)} %emission.3.terms_ref, bf16[256,640]{1,0:T(8,128)(2,1)S(1)} %constant_dynamic-update-slice_fusion.2.refs_0_, bf16[256,640]{1,0:T(8,128)(2,1)S(1)} %collective-permute-done.7.refs_1_, bf16[256,384]{1,0:T(8,128)(2,1)S(1)} %constant_dynamic-update-slice_fusion.refs_2_), custom_call_target="tpu_custom_call" | custom-call | flops 805306368 | bytes 1048576 | tf_op jit(solution)/shard_map/early/pallas_call | solution.py:211
  19.6 0.7 %collective-permute-done.6.refs_0_ = bf16[256,384]{1,0:T(8,128)(2,1)S(1)} collective-permute-done((bf16[256,384]{1,0:T(8,128)(2,1)S(1)}, bf16[256,384]{1,0:T(8,128)(2,1)S(1)}, u32[]{:S(2)}, u32[]{:S(2)}) %collective-permute-start.6) | collective-permute-done | bytes 196640 | tf_op jit(solution)/shard_map/ppermute | solution.py:235
  20.3 0.7 %image.1 = f32[16,24,128]{2,1,0:T(8,128)S(1)} custom-call(f32[1,9]{1,0:T(1,128)S(1)} %bitcast.16, bf16[288,2048]{1,0:T(8,128)(2,1)S(1)} %emission.3.terms_ref, f32[256,288]{1,0:T(8,128)S(1)} %early.1.given_ref, bf16[256,384]{1,0:T(8,128)(2,1)S(1)} %collective-permute-done.6.refs_0_), custom_call_target="tpu_custom_call" | custom-call | flops 268435456 | bytes 1048576 | tf_op jit(solution)/shard_map/image/pallas_call | solution.py:223
  21.1 12.3 %all_to_all.5 = f32[16,24,128]{2,1,0:T(8,128)S(1)} all-to-all(f32[16,24,128]{2,1,0:T(8,128)S(1)} %image.1), channel_id=1, replica_groups=mesh['groups'=2,'blk'=16] {'blk'}, dimensions={0} | all-to-all | bytes 393216 | tf_op jit(solution)/shard_map/all_to_all | solution.py:282
  33.4 0.1 fusion.4
  33.5 0.8 %copy_bitcast_fusion = f32[16,2048]{1,0:T(8,128)} fusion(f32[15,8,8]{2,1,0:T(8,128)S(1)} %get-tuple-element.30, f32[15,8,8]{2,1,0:T(8,128)S(1)} %get-tuple-element.31, f32[15,8,8]{2,1,0:T(8,128)S(1)} %get-tuple-element.32, f32[15,8,8]{2,1,0:T(8,128)S(1)} %get-tuple-element.29, f32[16,24,128]{2,1,0:T(8,128)S(1)} %all_to_all.5), kind=kLoop, calls=%fused_computation.3 | loop fusion | flops 589824 | bytes 507904 | tf_op jit(solution)/shard_map/reshape | solution.py:207
  (19 shorter events, 0.1 us)
Async XLA Ops:
  0.0 0.9 %copy-start = (bf16[128,512]{1,0:T(8,128)(2,1)S(1)}, bf16[128,512]{1,0:T(8,128)(2,1)}, u32[]{:S(2)}) copy-start(bf16[128,512]{1,0:T(8,128)(2,1)} %param.6) | copy-start | bytes 393220
  1.2 10.1 %collective-permute-start = (bf16[256,128]{1,0:T(8,128)(2,1)S(1)}, bf16[256,128]{1,0:T(8,128)(2,1)S(1)}, u32[]{:S(2)}, u32[]{:S(2)}) collective-permute-start(bf16[256,128]{1,0:T(8,128)(2,1)S(1)} %get-tuple-element.34), channel_id=1, source_target_pairs={{0,4},{1,5},{2,6},{3,7},{4,0},{5,1},{6,2},{7,3},{8,12},{9,13},{10,... | collective-permute-start | bytes 196616 | tf_op jit(solution)/shard_map/ppermute | solution.py:235
  4.2 7.3 %collective-permute-start.1 = (bf16[256,128]{1,0:T(8,128)(2,1)S(1)}, bf16[256,128]{1,0:T(8,128)(2,1)S(1)}, u32[]{:S(2)}, u32[]{:S(2)}) collective-permute-start(bf16[256,128]{1,0:T(8,128)(2,1)S(1)} %get-tuple-element.34), channel_id=1, source_target_pairs={{0,8},{1,9},{2,10},{3,11},{4,12},{5,13},{6,14},{7,15},{8,0},{9,1},... | collective-permute-start | bytes 196616 | tf_op jit(solution)/shard_map/ppermute | solution.py:235
  6.8 6.1 %collective-permute-start.2 = (bf16[256,128]{1,0:T(8,128)(2,1)S(1)}, bf16[256,128]{1,0:T(8,128)(2,1)S(1)}, u32[]{:S(2)}, u32[]{:S(2)}) collective-permute-start(bf16[256,128]{1,0:T(8,128)(2,1)S(1)} %get-tuple-element.34), channel_id=1, source_target_pairs={{0,12},{1,13},{2,14},{3,15},{4,8},{5,9},{6,10},{7,11},{8,4},{9,5},... | collective-permute-start | bytes 196616 | tf_op jit(solution)/shard_map/ppermute | solution.py:235
  6.8 6.1 %collective-permute-start.3 = (bf16[256,128]{1,0:T(8,128)(2,1)S(1)}, bf16[256,128]{1,0:T(8,128)(2,1)S(1)}, u32[]{:S(2)}, u32[]{:S(2)}) collective-permute-start(bf16[256,128]{1,0:T(8,128)(2,1)S(1)} %get-tuple-element.34), channel_id=1, source_target_pairs={{0,2},{1,3},{2,0},{3,1},{4,6},{5,7},{6,4},{7,5},{8,10},{9,11},{10,... | collective-permute-start | bytes 196616 | tf_op jit(solution)/shard_map/ppermute | solution.py:235
  8.6 0.7 %copy-start.4 = (f32[129]{0:T(256)S(1)}, f32[129]{0:T(256)}, u32[]{:S(2)}) copy-start(f32[129]{0:T(256)} %param.10) | copy-start | bytes 1552
  9.3 0.9 %copy-start.1 = (s32[32768]{0:T(1024)S(1)}, s32[32768]{0:T(1024)}, u32[]{:S(2)}) copy-start(s32[32768]{0:T(1024)} %param.8) | copy-start | bytes 393220
  9.3 1.0 %copy-start.2 = (f32[32768]{0:T(1024)S(1)}, f32[32768]{0:T(1024)}, u32[]{:S(2)}) copy-start(f32[32768]{0:T(1024)} %param.9) | copy-start | bytes 393220
  12.9 5.9 %collective-permute-start.4 = (bf16[256,256]{1,0:T(8,128)(2,1)S(1)}, bf16[256,256]{1,0:T(8,128)(2,1)S(1)}, u32[]{:S(2)}, u32[]{:S(2)}) collective-permute-start(bf16[256,256]{1,0:T(8,128)(2,1)S(1)} %pad_maximum_fusion), channel_id=1, source_target_pairs={{0,2},{1,3},{2,0},{3,1},{4,6},{5,7},{6,4},{7,5},{8,10},{9,11},{10,... | collective-permute-start | bytes 393224 | tf_op jit(solution)/shard_map/ppermute | solution.py:235
  14.5 4.3 %collective-permute-start.5 = (bf16[256,128]{1,0:T(8,128)(2,1)S(1)}, bf16[256,128]{1,0:T(8,128)(2,1)S(1)}, u32[]{:S(2)}, u32[]{:S(2)}) collective-permute-start(bf16[256,128]{1,0:T(8,128)(2,1)S(1)} %collective-permute-done.3), channel_id=1, source_target_pairs={{0,4},{1,5},{2,6},{3,7},{4,0},{5,1},{6,2},{7,3},{8,12},{9,13},{10,... | collective-permute-start | bytes 196616 | tf_op jit(solution)/shard_map/ppermute | solution.py:235
  14.6 4.3 %collective-permute-start.7 = (bf16[256,640]{1,0:T(8,128)(2,1)S(1)}, bf16[256,640]{1,0:T(8,128)(2,1)S(1)}, u32[]{:S(2)}, u32[]{:S(2)}) collective-permute-start(bf16[256,640]{1,0:T(8,128)(2,1)S(1)} %constant_dynamic-update-slice_fusion.2.refs_0_), channel_id=1, source_target_pairs={{0,1},{1,0},{2,3},{3,2},{4,5},{5,4},{6,7},{7,6},{8,9},{9,8},{10,11... | collective-permute-start | bytes 983048 | tf_op jit(solution)/shard_map/ppermute | solution.py:235
  18.8 1.5 %copy-start.3 = (f32[9]{0:T(128)S(1)}, f32[9]{0:T(128)}, u32[]{:S(2)}) copy-start(f32[9]{0:T(128)} %param.11) | copy-start | bytes 112
  18.8 1.5 %collective-permute-start.6 = (bf16[256,384]{1,0:T(8,128)(2,1)S(1)}, bf16[256,384]{1,0:T(8,128)(2,1)S(1)}, u32[]{:S(2)}, u32[]{:S(2)}) collective-permute-start(bf16[256,384]{1,0:T(8,128)(2,1)S(1)} %constant_dynamic-update-slice_fusion.refs_2_), channel_id=1, source_target_pairs={{0,1},{1,0},{2,3},{3,2},{4,5},{5,4},{6,7},{7,6},{8,9},{9,8},{10,11... | collective-permute-start | bytes 589832 | tf_op jit(solution)/shard_map/ppermute | solution.py:235
